TPU v7x, 128 devices: a whole 4x4x4 slice. The times are simulated.
128 devices in a mesh: gx: 32 (over y, x, core), gy: 4 (over z).
Axes of the slice: x: 4, y: 4, z: 4, core: 2. Of those that a mesh axis runs over, the one named last changes fastest.
Arguments:
- hidden_in: bfloat16 [1024, 16384], P(('gx', 'gy')), may hold values from -6 to 6
- norm_gain: float32 [16384], replicated, may hold values from 0.1 to 1.9
- w_qkv: bfloat16 [16384, 18432], P('gy', 'gx'), may hold values from -0.046875 to 0.046875
- k_cache: bfloat16 [1024, 512, 1024], P(('gx', 'gy')), may hold values from -60 to 60
- v_cache: bfloat16 [1024, 512, 1024], P(('gx', 'gy')), may hold values from -6 to 6
- lengths: int32 [1024], P(('gx', 'gy')), may hold values from 1 to 512, as said below
- w_out: bfloat16 [16384, 16384], P('gy', 'gx'), may hold values from -0.375 to 0.375
Outputs:
- attn_out: bfloat16 [1024, 16384], P(('gx', 'gy'))
Inputs may be any that keep to these rules, and one draw needn't show every extreme that they name: Row b attends to its first lengths[b] cached positions; some row has 512.
All inputs are finite; a program needn't handle non-finite values.
Results may differ from a plain program's by a relative error of at most 0.015.
The roundings to bfloat16 on the way count: a program that leaves them out, or rounds other values in their place, can miss the bound.
Values may be sent and summed in bfloat16 or wider, within the bound.
A program may use at most 128 MiB of HBM per device.

v0:
```python
import math

import jax
import jax.numpy as jnp
from jax import lax
from jax.sharding import PartitionSpec as P

HQ = 128
KVH = 8
HD = 128


eps = 1e-05
theta = 500000.0


def rotate(values, position, head_size):
    half = head_size // 2
    index = jnp.arange(half, dtype=jnp.float32)
    freqs = theta ** (-2.0 * index / head_size)
    angle = position[:, None, None] * freqs[None, None, :]
    cosine = jnp.cos(angle)
    sine = jnp.sin(angle)
    first = values[..., :half]
    second = values[..., half:]
    return jnp.concatenate(
        [first * cosine - second * sine, second * cosine + first * sine], axis=-1
    )


def normalize(scores, fresh):
    top = jnp.maximum(jnp.max(scores, axis=-1), fresh)
    probs = jnp.exp(scores - top[..., None])
    pnew = jnp.exp(fresh - top)
    total = jnp.sum(probs, axis=-1) + pnew
    return ((probs / total[..., None]).astype(jnp.bfloat16), (pnew / total).astype(jnp.bfloat16))


def attend_local(owned, k_cache, v_cache, lengths):
    rows = owned.shape[0]
    span = k_cache.shape[1]
    share = HQ // KVH
    query = owned[:, : HQ * HD].reshape(rows, HQ, HD).astype(jnp.float32)
    key_new = owned[:, HQ * HD : (HQ + KVH) * HD].reshape(rows, KVH, HD).astype(jnp.float32)
    value_new = owned[:, (HQ + KVH) * HD :].reshape(rows, KVH, HD).astype(jnp.float32)
    position = lengths.astype(jnp.float32)
    grouped = rotate(query, position, HD).astype(jnp.bfloat16).reshape(rows, KVH, share, HD)
    key_new = rotate(key_new, position, HD).astype(jnp.bfloat16)
    keys = k_cache.reshape(rows, span, KVH, HD)
    values = v_cache.reshape(rows, span, KVH, HD)
    scale = 1.0 / math.sqrt(HD)
    fresh = (
        jnp.einsum("rgsd,rgd->rgs", grouped, key_new, preferred_element_type=jnp.float32) * scale
    )
    scores = (
        jnp.einsum("rgsd,rtgd->rgst", grouped, keys, preferred_element_type=jnp.float32) * scale
    )
    valid = jnp.arange(span, dtype=jnp.int32)[None, :] < lengths[:, None]
    scores = jnp.where(valid[:, None, None, :], scores, -jnp.inf)
    weights, wnew = normalize(scores, fresh)
    mixed = jnp.einsum("rgst,rtgd->rgsd", weights, values, preferred_element_type=jnp.float32)
    mixed = mixed + wnew.astype(jnp.float32)[..., None] * value_new[:, :, None, :]
    return mixed.reshape(rows, HQ * HD).astype(jnp.bfloat16)


def on_device(hidden_in, norm_gain, w_qkv, k_cache, v_cache, lengths, w_out):
    widened = hidden_in.astype(jnp.float32)
    normed = (
        widened * lax.rsqrt(jnp.mean(widened * widened, axis=-1, keepdims=True) + eps) * norm_gain
    ).astype(jnp.bfloat16)
    grouped_in = lax.all_gather(normed, "gx", axis=0, tiled=True)
    spread_in = lax.all_to_all(grouped_in, "gy", split_axis=1, concat_axis=0, tiled=True)
    picked = spread_in
    partial_qkv = lax.psum_scatter(
        jnp.dot(picked, w_qkv, preferred_element_type=jnp.float32),
        "gy",
        scatter_dimension=0,
        tiled=True,
    )
    owned = lax.all_to_all(
        partial_qkv.astype(jnp.bfloat16), "gx", split_axis=0, concat_axis=1, tiled=True
    )
    attended = attend_local(owned, k_cache, v_cache, lengths)
    grouped_out = lax.all_gather(attended, "gx", axis=0, tiled=True)
    spread_out = lax.all_to_all(grouped_out, "gy", split_axis=1, concat_axis=0, tiled=True)
    picked = spread_out
    partial_out = lax.psum_scatter(
        jnp.dot(picked, w_out, preferred_element_type=jnp.float32).astype(jnp.bfloat16),
        "gy",
        scatter_dimension=0,
        tiled=True,
    )
    return lax.all_to_all(partial_out, "gx", split_axis=0, concat_axis=1, tiled=True)


def solution(mesh):
    return jax.shard_map(
        on_device,
        mesh=mesh,
        in_specs=(
            P(("gx", "gy"), None),
            P(),
            P("gy", "gx"),
            P(("gx", "gy"), None, None),
            P(("gx", "gy"), None, None),
            P(("gx", "gy")),
            P("gy", "gx"),
        ),
        out_specs=P(("gx", "gy"), None),
        check_vma=False,
    )
```

profile of v0, /device:TPU:1, one launch (start us, length us, event | category | flops | bytes accessed | tf_op | source)
XLA Modules:
  0.0 490.7 jit_solution(18426097458056642871)
XLA Ops:
  6.5 0.0 all-gather.3.cloned.1.call-start
  6.5 1.2 fusion.19
  7.7 1.8 fusion.21
  9.5 0.0 all-gather.3.cloned.1.call-update
  9.6 0.0 reduce-scatter.3.cloned.1.call-start
  9.6 56.5 %all-gather.3.cloned.1.call-done = bf16[256,16384]{1,0:T(8,128)(2,1)} async-done(((bf16[8,16384]{1,0:T(8,128)(2,1)}), bf16[256,16384]{1,0:T(8,128)(2,1)}) %all-gather.3.cloned.1.call-update) | async-done | bytes 8388624 | tf_op jit(solution)/shard_map/all_gather | solution.py:71
  66.1 12.0 %copy.31 = bf16[256,16384]{0,1:T(8,128)(2,1)} copy(bf16[256,16384]{1,0:T(8,128)(2,1)} %all-gather.3.cloned.1.call-done) | data formatting | bytes 16777216 | tf_op jit(solution)/shard_map/all_gather | solution.py:71
  78.1 101.0 %all_to_all.76 = bf16[256,4,4096]{0,2,1:T(8,128)(2,1)} all-to-all(bf16[256,4,4096]{0,2,1:T(8,128)(2,1)} %bitcast.62), channel_id=1, replica_groups=mesh['gx'=32,'gy'=4] {'gy'}, dimensions={1} | all-to-all | bytes 16777216 | tf_op jit(solution)/shard_map/all_to_all | solution.py:72
  179.1 11.3 %copy.32 = bf16[4,256,4096]{2,1,0:T(8,128)(2,1)} copy(bf16[4,256,4096]{1,2,0:T(8,128)(2,1)} %bitcast.63) | data formatting | bytes 16777216 | tf_op jit(solution)/shard_map/all_to_all | solution.py:72
  190.4 0.0 copy-start
  190.4 10.4 %fusion.34 = f32[1024,576]{0,1:T(8,128)} fusion(bf16[1024,4096]{1,0:T(8,128)(2,1)} %bitcast.66, bf16[4096,576]{0,1:T(8,128)(2,1)} %param.9), kind=kOutput, calls=%fused_computation.54 | convolution fusion | flops 4831838208 | bytes 15466496 | tf_op jit(solution)/shard_map/dot_general | solution.py:75
  200.8 0.0 reduce-scatter.3.cloned.1.call-update
  200.8 0.0 copy-done
  200.9 0.1 iota_compare_fusion
  200.9 30.3 %reduce-scatter.3.cloned.1.call-done = f32[256,576]{0,1:T(8,128)} async-done(((f32[1024,576]{0,1:T(8,128)}), f32[256,576]{0,1:T(8,128)}) %reduce-scatter.3.cloned.1.call-update) | async-done | bytes 589840 | tf_op jit(solution)/shard_map/reduce_scatter | solution.py:74
  231.2 1.1 convert_element_type.57
  232.3 0.9 copy.33
  233.2 7.5 %all-to-all-start.1 = ((bf16[32,8,576]{2,1,0:T(8,128)(2,1)}), bf16[32,8,576]{2,1,0:T(8,128)(2,1)S(1)}, u32[]{:S(2)}, u32[]{:S(2)}) async-start(bf16[32,8,576]{2,1,0:T(8,128)(2,1)} %bitcast.3), calls=%async_computation.2 | async-start | bytes 655360 | tf_op jit(solution)/shard_map/all_to_all | solution.py:80
  240.7 0.0 all-gather.5.cloned.1.call-start
  240.8 0.1 multiply_cosine_fusion
  240.9 9.4 %all-to-all-done.1 = bf16[32,8,576]{2,1,0:T(8,128)(2,1)S(1)} async-done(((bf16[32,8,576]{2,1,0:T(8,128)(2,1)}), bf16[32,8,576]{2,1,0:T(8,128)(2,1)S(1)}, u32[]{:S(2)}, u32[]{:S(2)}) %all-to-all-start.1) | async-done | bytes 294944 | tf_op jit(solution)/shard_map/all_to_all | solution.py:80
  250.3 0.3 all_to_all.63
  250.7 0.2 fusion.33
  250.9 0.1 subtract_convert_fusion.1
  251.0 0.1 maximum_bitcast_fusion
  251.0 0.0 slice-start
  251.0 0.2 subtract_convert_fusion
  251.3 0.3 fusion.23
  251.6 0.0 slice-start.1
  251.6 6.1 %fusion.6 = (f32[8,8,16]{2,1,0:T(8,128)S(1)}, f32[8,8,16,512]{3,2,1,0:T(8,128)S(1)}) fusion(pred[8,512]{1,0:T(8,128)(4,1)S(1)} %iota_compare_fusion, bf16[8,8,16,64]{3,2,1,0:T(8,128)(2,1)S(1)} %bitcast.72, bf16[8,8,16,64]{3,2,1,0:T(8,128)(2,1)S(1)} %bitcast.70, bf16[8,512,1024]{2,1,0:T(8,128)(2,1)} %param.10), kind=kOutput, calls=%fused_computation.9 | convolution fusion | flops 136313856 | bytes 10756096 | tf_op jit(solution)/shard_map/rgsd,rtgd->rgst/dot_general | solution.py:56
  257.7 0.6 fusion.7
  258.4 0.0 slice-done
  258.4 0.0 slice-done.1
  258.4 2.1 fusion.11
  260.6 0.9 copy.70
  261.4 0.0 all-gather.5.cloned.1.call-update
  261.5 0.0 reduce-scatter.5.cloned.1.call-start
  261.5 49.1 %all-gather.5.cloned.1.call-done = bf16[256,16384]{1,0:T(8,128)(2,1)} async-done(((bf16[8,16384]{1,0:T(8,128)(2,1)}), bf16[256,16384]{1,0:T(8,128)(2,1)}) %all-gather.5.cloned.1.call-update) | async-done | bytes 8388624 | tf_op jit(solution)/shard_map/all_gather | solution.py:84
  310.6 12.0 %copy.40 = bf16[256,16384]{0,1:T(8,128)(2,1)} copy(bf16[256,16384]{1,0:T(8,128)(2,1)} %all-gather.5.cloned.1.call-done) | data formatting | bytes 16777216 | tf_op jit(solution)/shard_map/all_gather | solution.py:84
  322.6 101.0 %all_to_all.77 = bf16[256,4,4096]{0,2,1:T(8,128)(2,1)} all-to-all(bf16[256,4,4096]{0,2,1:T(8,128)(2,1)} %bitcast.64), channel_id=1, replica_groups=mesh['gx'=32,'gy'=4] {'gy'}, dimensions={1} | all-to-all | bytes 16777216 | tf_op jit(solution)/shard_map/all_to_all | solution.py:85
  423.6 11.3 %copy.41 = bf16[4,256,4096]{2,1,0:T(8,128)(2,1)} copy(bf16[4,256,4096]{1,2,0:T(8,128)(2,1)} %bitcast.65) | data formatting | bytes 16777216 | tf_op jit(solution)/shard_map/all_to_all | solution.py:85
  434.9 10.1 %convolution_convert_fusion = bf16[1024,512]{1,0:T(8,128)(2,1)} fusion(bf16[1024,4096]{1,0:T(8,128)(2,1)} %bitcast.67, bf16[4096,512]{1,0:T(8,128)(2,1)} %param.13), kind=kOutput, calls=%fused_computation.11 | convolution fusion | flops 4295491584 | bytes 13631488 | tf_op jit(solution)/shard_map/dot_general | solution.py:88
  445.0 0.0 reduce-scatter.5.cloned.1.call-update
  445.0 20.2 %reduce-scatter.5.cloned.1.call-done = bf16[256,512]{1,0:T(8,128)(2,1)} async-done(((bf16[1024,512]{1,0:T(8,128)(2,1)}), bf16[256,512]{1,0:T(8,128)(2,1)}) %reduce-scatter.5.cloned.1.call-update) | async-done | bytes 262160 | tf_op jit(solution)/shard_map/reduce_scatter | solution.py:87
  465.3 18.2 %all_to_all.78 = bf16[32,8,512]{2,1,0:T(8,128)(2,1)S(1)} all-to-all(bf16[32,8,512]{2,1,0:T(8,128)(2,1)} %bitcast.75), channel_id=1, replica_groups=mesh['gx'=32,'gy'=4] {'gx'}, dimensions={0} | all-to-all | bytes 524288 | tf_op jit(solution)/shard_map/all_to_all | solution.py:93
  483.5 0.7 copy.72
  (10 shorter events, 0.2 us)
Async XLA Ops:
  6.5 59.6 %all-gather.3.cloned.1.call-start = ((), (), s32[]{:S(2)}) async-start(), calls=%async_computation.6 | async-start | bytes 8650752 | tf_op jit(solution)/shard_map/all_gather | solution.py:71
  9.6 221.6 %reduce-scatter.3.cloned.1.call-start = ((), (), s32[]{:S(2)}) async-start(), calls=%async_computation.7 | async-start | bytes 2949120 | tf_op jit(solution)/shard_map/reduce_scatter | solution.py:74
  190.4 10.5 %copy-start = (s32[8]{0:T(128)S(1)}, s32[8]{0:T(128)}, u32[]{:S(2)}) copy-start(s32[8]{0:T(128)} %param.12) | copy-start | bytes 100
  233.2 17.0 %all-to-all-start.1 = ((bf16[32,8,576]{2,1,0:T(8,128)(2,1)}), bf16[32,8,576]{2,1,0:T(8,128)(2,1)S(1)}, u32[]{:S(2)}, u32[]{:S(2)}) async-start(bf16[32,8,576]{2,1,0:T(8,128)(2,1)} %bitcast.3), calls=%async_computation.2 | async-start | bytes 655360 | tf_op jit(solution)/shard_map/all_to_all | solution.py:80
  240.7 69.9 %all-gather.5.cloned.1.call-start = ((), (), s32[]{:S(2)}) async-start(), calls=%async_computation.8 | async-start | bytes 8650752 | tf_op jit(solution)/shard_map/all_gather | solution.py:84
  251.0 7.3 %slice-start = ((s8[8388608]{0:T(1024)(128)(4,1)}), s8[4194304]{0:T(1024)(128)(4,1)S(1)}, s32[]{:S(2)}) async-start(s8[8388608]{0:T(1024)(128)(4,1)} %bitcast.79), calls=%async_computation.10 | async-start | bytes 8388608
  251.6 6.8 %slice-start.1 = ((s8[8388608]{0:T(1024)(128)(4,1)}), s8[4194304]{0:T(1024)(128)(4,1)S(1)}, s32[]{:S(2)}) async-start(s8[8388608]{0:T(1024)(128)(4,1)} %bitcast.79), calls=%async_computation.11 | async-start | bytes 8388608
  261.5 203.8 %reduce-scatter.5.cloned.1.call-start = ((), (), s32[]{:S(2)}) async-start(), calls=%async_computation.9 | async-start | bytes 1310720 | tf_op jit(solution)/shard_map/reduce_scatter | solution.py:87
Sparse Core Ops, SparseCore 0:
  9.7 56.3 all-gather.2
  201.0 30.1 reduce-scatter.2
  261.6 48.9 all-gather.4
  445.1 20.0 reduce-scatter.4
where the time goes:
time: 492 us; the launch traced here: 491 us
  blocking collectives  220 us (45%)
  waiting for transfers between devices  166 us (34%)
  local copies, waits for them, and re-layouts  49.6 us (10%)
  matrix products  29.1 us (6%)
  between operations  13.3 us (3%)
  starting transfers between devices  7.61 us (2%)
  other arithmetic  5.39 us (1%)
    all_to_all x1, blocking collectives, on_device(): lax.all_to_all(grouped_in, 'gy', split_axis=1, concat_axis=0, tiled=True)  101 us
    all_to_all x1, blocking collectives, on_device(): lax.all_to_all(grouped_out, 'gy', split_axis=1, concat_axis=0, tiled=True)  101 us
    all_gather x1, waiting for transfers between devices, on_device(): grouped_in = lax.all_gather(normed, 'gx', axis=0, tiled=True)  56.5 us
    all_gather x1, waiting for transfers between devices, on_device(): grouped_out = lax.all_gather(attended, 'gx', axis=0, tiled=True)  49.1 us
    reduce_scatter x1, waiting for transfers between devices, on_device(): lax.psum_scatter(jnp.dot(picked, w_qkv, preferred_element_type=jnp.float3...  30.3 us
    reduce_scatter x1, waiting for transfers between devices, on_device(): lax.psum_scatter(jnp.dot(picked, w_out, preferred_element_type=jnp.float3...  20.2 us
    all_to_all x1, blocking collectives, on_device(): lax.all_to_all(partial_out, 'gx', split_axis=0, concat_axis=1, tiled=True)  18.2 us
    all_gather x1, local copies, waits for them, and re-layouts, on_device(): grouped_in = lax.all_gather(normed, 'gx', axis=0, tiled=True)  12 us
  transfers between devices with their start and end apart: 5, of which 5 were waited for; matrix products, arithmetic and copies ran while one was open for 0% of the time, Pallas kernels for 0%

commit v1 on v0

--- a/solution.py
+++ b/solution.py
@@ -63,16 +63,22 @@
     return mixed.reshape(rows, HQ * HD).astype(jnp.bfloat16)
 
 
+def gather_rows(rows):
+    blocks = rows.reshape(rows.shape[0], 4, -1).transpose(1, 0, 2)
+    spread = lax.all_to_all(blocks, "gy", split_axis=0, concat_axis=0, tiled=True)
+    return lax.all_gather(spread.reshape(32, -1), "gx", axis=0, tiled=True)
+
+
 def on_device(hidden_in, norm_gain, w_qkv, k_cache, v_cache, lengths, w_out):
     widened = hidden_in.astype(jnp.float32)
     normed = (
         widened * lax.rsqrt(jnp.mean(widened * widened, axis=-1, keepdims=True) + eps) * norm_gain
     ).astype(jnp.bfloat16)
-    grouped_in = lax.all_gather(normed, "gx", axis=0, tiled=True)
-    spread_in = lax.all_to_all(grouped_in, "gy", split_axis=1, concat_axis=0, tiled=True)
-    picked = spread_in
+    picked = gather_rows(normed)
     partial_qkv = lax.psum_scatter(
-        jnp.dot(picked, w_qkv, preferred_element_type=jnp.float32),
+        jnp.dot(picked, w_qkv, preferred_element_type=jnp.float32).reshape(32, 4, 8, -1)
+        .transpose(1, 0, 2, 3)
+        .reshape(1024, -1),
         "gy",
         scatter_dimension=0,
         tiled=True,
@@ -81,11 +87,13 @@
         partial_qkv.astype(jnp.bfloat16), "gx", split_axis=0, concat_axis=1, tiled=True
     )
     attended = attend_local(owned, k_cache, v_cache, lengths)
-    grouped_out = lax.all_gather(attended, "gx", axis=0, tiled=True)
-    spread_out = lax.all_to_all(grouped_out, "gy", split_axis=1, concat_axis=0, tiled=True)
-    picked = spread_out
+    picked = gather_rows(attended)
     partial_out = lax.psum_scatter(
-        jnp.dot(picked, w_out, preferred_element_type=jnp.float32).astype(jnp.bfloat16),
+        jnp.dot(picked, w_out, preferred_element_type=jnp.float32)
+        .astype(jnp.bfloat16)
+        .reshape(32, 4, 8, -1)
+        .transpose(1, 0, 2, 3)
+        .reshape(1024, -1),
         "gy",
         scatter_dimension=0,
         tiled=True,

time: 492 us -> 266 us (0.54)
  blocking collectives: 220 us -> 39.3 us
  local copies, waits for them, and re-layouts: 49.6 us -> 4.26 us
    all_to_all x2, blocking collectives: 202 us -> 20.9 us  [gather_rows(): lax.all_to_all(blocks, 'gy', split_axis=0, concat_axis=0, tiled=True)]
    all_gather x2 -> x0, local copies, waits for them, and re-layouts: 23.9 us -> none  [the longest x1 12 us: on_device(): grouped_in = lax.all_gather(normed, 'gx', axis=0, tiled=True)]
    all_to_all x2 -> x0, local copies, waits for them, and re-layouts: 22.6 us -> none  [the longest x1 11.3 us: on_device(): lax.all_to_all(grouped_in, 'gy', split_axis=1, concat_axis=0, tiled=True)]
where the time goes in v1:
time: 266 us
  waiting for transfers between devices  168 us (63%)
  blocking collectives  39.3 us (15%)
  matrix products  28.1 us (11%)
  between operations  13.3 us (5%)
  starting transfers between devices  7.77 us (3%)
  other arithmetic  5.45 us (2%)
  local copies, waits for them, and re-layouts  4.26 us (2%)
    all_gather x2, waiting for transfers between devices, gather_rows(): return lax.all_gather(spread.reshape(32, -1), 'gx', axis=0, tiled=True)  104 us
    reduce_scatter x1, waiting for transfers between devices, on_device(): lax.psum_scatter(jnp.dot(picked, w_qkv, preferred_element_type=jnp.float3...  33.5 us
    reduce_scatter x1, waiting for transfers between devices, on_device(): lax.psum_scatter(jnp.dot(picked, w_out, preferred_element_type=jnp.float3...  21.1 us
    all_to_all x2, blocking collectives, gather_rows(): lax.all_to_all(blocks, 'gy', split_axis=0, concat_axis=0, tiled=True)  20.9 us
    all_to_all x1, blocking collectives, on_device(): lax.all_to_all(partial_out, 'gx', split_axis=0, concat_axis=1, tiled=True)  18.5 us
    dot_general x1, matrix products, on_device(): jnp.dot(picked, w_qkv, preferred_element_type=jnp.float32)  10.5 us
    all_to_all x1, waiting for transfers between devices, on_device(): lax.all_to_all(partial_qkv.astype(jnp.bfloat16), 'gx', split_axis=0, conc...  9.36 us
    dot_general x1, matrix products, on_device(): jnp.dot(picked, w_out, preferred_element_type=jnp.float32)  9.07 us
  transfers between devices with their start and end apart: 5, of which 5 were waited for; matrix products, arithmetic and copies ran while one was open for 0% of the time, Pallas kernels for 0%

profile of v1, /device:TPU:1, one launch (start us, length us, event | category | flops | bytes accessed | tf_op | source)
XLA Modules:
  0.0 266.0 jit_solution(7116271638651803321)
XLA Ops:
  6.5 0.0 all-gather.3.cloned.1.call-start
  6.5 1.2 fusion.19
  7.7 1.1 fusion.21
  8.8 11.3 %all_to_all.48 = bf16[4,8,4096]{2,1,0:T(8,128)(2,1)} all-to-all(bf16[4,8,4096]{2,1,0:T(8,128)(2,1)S(1)} %bitcast.83), channel_id=1, replica_groups=mesh['gx'=32,'gy'=4] {'gy'}, dimensions={0} | all-to-all | bytes 524288 | tf_op jit(solution)/shard_map/all_to_all | solution.py:68
  20.2 0.0 all-gather.3.cloned.1.call-update
  20.2 0.0 reduce-scatter.3.cloned.1.call-start
  20.2 54.2 %all-gather.3.cloned.1.call-done = bf16[1024,4096]{1,0:T(8,128)(2,1)} async-done(((bf16[32,4096]{1,0:T(8,128)(2,1)}), bf16[1024,4096]{1,0:T(8,128)(2,1)}) %all-gather.3.cloned.1.call-update) | async-done | bytes 8388624 | tf_op jit(solution)/shard_map/all_gather | solution.py:69
  74.4 10.5 %fusion.34 = f32[1024,576]{1,0:T(8,128)S(1)} fusion(bf16[1024,4096]{1,0:T(8,128)(2,1)} %all-gather.3.cloned.1.call-done, bf16[4096,576]{0,1:T(8,128)(2,1)} %param.9), kind=kOutput, calls=%fused_computation.55 | convolution fusion | flops 4831838208 | bytes 15466496 | tf_op jit(solution)/shard_map/dot_general | solution.py:79
  85.0 0.0 copy-start
  85.0 1.7 copy.17
  86.7 0.0 reduce-scatter.3.cloned.1.call-update
  86.7 0.0 copy-done
  86.7 0.1 iota_compare_fusion
  86.8 33.5 %reduce-scatter.3.cloned.1.call-done = f32[256,576]{1,0:T(8,128)} async-done(((f32[1024,576]{1,0:T(8,128)}), f32[256,576]{1,0:T(8,128)}) %reduce-scatter.3.cloned.1.call-update) | async-done | bytes 589840 | tf_op jit(solution)/shard_map/reduce_scatter | solution.py:78
  120.3 1.8 convert_bitcast_fusion
  122.2 7.5 %all-to-all-start.1 = ((bf16[32,8,576]{2,1,0:T(8,128)(2,1)}), bf16[32,8,576]{2,1,0:T(8,128)(2,1)S(1)}, u32[]{:S(2)}, u32[]{:S(2)}) async-start(bf16[32,8,576]{2,1,0:T(8,128)(2,1)} %convert_bitcast_fusion), calls=%async_computation.2 | async-start | bytes 655360 | tf_op jit(solution)/shard_map/all_to_all | solution.py:86
  129.6 0.0 all-gather.5.cloned.1.call-start
  129.7 0.1 multiply_cosine_fusion
  129.8 9.4 %all-to-all-done.1 = bf16[32,8,576]{2,1,0:T(8,128)(2,1)S(1)} async-done(((bf16[32,8,576]{2,1,0:T(8,128)(2,1)}), bf16[32,8,576]{2,1,0:T(8,128)(2,1)S(1)}, u32[]{:S(2)}, u32[]{:S(2)}) %all-to-all-start.1) | async-done | bytes 294944 | tf_op jit(solution)/shard_map/all_to_all | solution.py:86
  139.2 0.3 all_to_all.38
  139.6 0.2 fusion.33
  139.8 0.1 subtract_convert_fusion.1
  139.9 0.1 maximum_bitcast_fusion
  140.0 0.0 slice-start
  140.0 0.2 subtract_convert_fusion
  140.2 0.3 fusion.23
  140.5 0.0 slice-start.1
  140.5 6.1 %fusion.6 = (f32[8,8,16]{2,1,0:T(8,128)S(1)}, f32[8,8,16,512]{3,2,1,0:T(8,128)S(1)}) fusion(pred[8,512]{1,0:T(8,128)(4,1)S(1)} %iota_compare_fusion, bf16[8,8,16,64]{3,2,1,0:T(8,128)(2,1)S(1)} %bitcast.79, bf16[8,8,16,64]{3,2,1,0:T(8,128)(2,1)S(1)} %bitcast.77, bf16[8,512,1024]{2,1,0:T(8,128)(2,1)} %param.10), kind=kOutput, calls=%fused_computation.9 | convolution fusion | flops 136313856 | bytes 10756096 | tf_op jit(solution)/shard_map/rgsd,rtgd->rgst/dot_general | solution.py:56
  146.6 0.7 fusion.7
  147.3 0.0 slice-done
  147.3 0.0 slice-done.1
  147.3 2.2 fusion.11
  149.5 0.1 convert_element_type.70
  149.6 0.2 copy.54
  149.7 9.6 %all_to_all.49 = bf16[4,8,4096]{2,1,0:T(8,128)(2,1)} all-to-all(bf16[4,8,4096]{2,1,0:T(8,128)(2,1)S(1)} %bitcast.81), channel_id=1, replica_groups=mesh['gx'=32,'gy'=4] {'gy'}, dimensions={0} | all-to-all | bytes 524288 | tf_op jit(solution)/shard_map/all_to_all | solution.py:68
  159.3 0.0 all-gather.5.cloned.1.call-update
  159.3 0.2 reduce-scatter.5.cloned.1.call-start
  159.5 49.5 %all-gather.5.cloned.1.call-done = bf16[1024,4096]{1,0:T(8,128)(2,1)} async-done(((bf16[32,4096]{1,0:T(8,128)(2,1)}), bf16[1024,4096]{1,0:T(8,128)(2,1)}) %all-gather.5.cloned.1.call-update) | async-done | bytes 8388624 | tf_op jit(solution)/shard_map/all_gather | solution.py:69
  209.0 9.1 %convolution_convert_fusion = bf16[1024,512]{1,0:T(8,128)(2,1)S(1)} fusion(bf16[1024,4096]{1,0:T(8,128)(2,1)} %all-gather.5.cloned.1.call-done, bf16[4096,512]{1,0:T(8,128)(2,1)} %param.13), kind=kOutput, calls=%fused_computation.11 | convolution fusion | flops 4295491584 | bytes 13631488 | tf_op jit(solution)/shard_map/dot_general | solution.py:92
  218.1 1.1 copy.25
  219.2 0.0 reduce-scatter.5.cloned.1.call-update
  219.2 21.1 %reduce-scatter.5.cloned.1.call-done = bf16[256,512]{1,0:T(8,128)(2,1)} async-done(((bf16[1024,512]{1,0:T(8,128)(2,1)}), bf16[256,512]{1,0:T(8,128)(2,1)}) %reduce-scatter.5.cloned.1.call-update) | async-done | bytes 262160 | tf_op jit(solution)/shard_map/reduce_scatter | solution.py:91
  240.3 18.5 %all_to_all.50 = bf16[32,8,512]{2,1,0:T(8,128)(2,1)S(1)} all-to-all(bf16[32,8,512]{2,1,0:T(8,128)(2,1)} %bitcast.84), channel_id=1, replica_groups=mesh['gx'=32,'gy'=4] {'gx'}, dimensions={0} | all-to-all | bytes 524288 | tf_op jit(solution)/shard_map/all_to_all | solution.py:101
  258.7 0.7 copy.56
  (10 shorter events, 0.2 us)
Async XLA Ops:
  6.5 67.9 %all-gather.3.cloned.1.call-start = ((), (), s32[]{:S(2)}) async-start(), calls=%async_computation.6 | async-start | bytes 8650752 | tf_op jit(solution)/shard_map/all_gather | solution.py:69
  20.2 100.1 %reduce-scatter.3.cloned.1.call-start = ((), (), s32[]{:S(2)}) async-start(), calls=%async_computation.7 | async-start | bytes 3276800 | tf_op jit(solution)/shard_map/reduce_scatter | solution.py:78
  85.0 1.7 copy-start
  122.2 17.0 %all-to-all-start.1 = ((bf16[32,8,576]{2,1,0:T(8,128)(2,1)}), bf16[32,8,576]{2,1,0:T(8,128)(2,1)S(1)}, u32[]{:S(2)}, u32[]{:S(2)}) async-start(bf16[32,8,576]{2,1,0:T(8,128)(2,1)} %convert_bitcast_fusion), calls=%async_computation.2 | async-start | bytes 655360 | tf_op jit(solution)/shard_map/all_to_all | solution.py:86
  129.6 79.4 %all-gather.5.cloned.1.call-start = ((), (), s32[]{:S(2)}) async-start(), calls=%async_computation.8 | async-start | bytes 8650752 | tf_op jit(solution)/shard_map/all_gather | solution.py:69
  140.0 7.3 %slice-start = ((s8[8388608]{0:T(1024)(128)(4,1)}), s8[4194304]{0:T(1024)(128)(4,1)S(1)}, s32[]{:S(2)}) async-start(s8[8388608]{0:T(1024)(128)(4,1)} %bitcast.87), calls=%async_computation.10 | async-start | bytes 8388608
  140.5 6.8 %slice-start.1 = ((s8[8388608]{0:T(1024)(128)(4,1)}), s8[4194304]{0:T(1024)(128)(4,1)S(1)}, s32[]{:S(2)}) async-start(s8[8388608]{0:T(1024)(128)(4,1)} %bitcast.87), calls=%async_computation.11 | async-start | bytes 8388608
  159.3 81.0 %reduce-scatter.5.cloned.1.call-start = ((), (), s32[]{:S(2)}) async-start(), calls=%async_computation.9 | async-start | bytes 1310720 | tf_op jit(solution)/shard_map/reduce_scatter | solution.py:91
Sparse Core Ops, SparseCore 0:
  20.3 54.0 all-gather.2
  86.8 33.4 reduce-scatter.2
  159.4 49.5 all-gather.4
  219.3 20.8 reduce-scatter.4

commit v2 on v0

--- a/solution.py
+++ b/solution.py
@@ -1,17 +1,449 @@
+import functools
 import math
 
 import jax
 import jax.numpy as jnp
 from jax import lax
+from jax.experimental import pallas as pl
+from jax.experimental.pallas import tpu as pltpu
 from jax.sharding import PartitionSpec as P
 
 HQ = 128
 KVH = 8
 HD = 128
-
+DEPTH = 4096
+QWIDE = 640
 
 eps = 1e-05
 theta = 500000.0
+
+UNITS = (
+    ((0, 0), (0, 3), (0, 1), (0, 2)),
+    ((1, 0), (3, 0), (1, 3), (3, 3)),
+    ((1, 1), (3, 1), (1, 2), (3, 2)),
+    ((2, 0), (2, 3), (2, 1), (2, 2)),
+)
+PLACE = {ur: (w, i) for w, unit in enumerate(UNITS) for i, ur in enumerate(unit)}
+
+
+def remote(src, dst, send, recv, device):
+    return pltpu.make_async_remote_copy(
+        src_ref=src,
+        dst_ref=dst,
+        send_sem=send,
+        recv_sem=recv,
+        device_id=device,
+        device_id_type=pl.DeviceIdType.MESH,
+    )
+
+
+class Here:
+    def __init__(self):
+        gx = lax.axis_index("gx")
+        self.gx = gx
+        self.z = lax.axis_index("gy")
+        self.y = gx // 8
+        self.x = (gx // 2) % 4
+        self.c = gx % 2
+
+    def device(self, dy=0, dx=0, dc=0, dz=0):
+        y = (self.y + dy) % 4
+        x = (self.x + dx) % 4
+        c = (self.c + dc) % 2
+        return ((y * 4 + x) * 2 + c, (self.z + dz) % 4)
+
+    def greet(self):
+        barrier = pltpu.get_barrier_semaphore()
+        for dy in range(4):
+            for dx in range(4):
+                for dc in range(2):
+                    if dy or dx or dc:
+                        pl.semaphore_signal(
+                            barrier,
+                            inc=1,
+                            device_id=self.device(dy, dx, dc),
+                            device_id_type=pl.DeviceIdType.MESH,
+                        )
+        for dz in range(1, 4):
+            pl.semaphore_signal(
+                barrier,
+                inc=1,
+                device_id=self.device(dz=dz),
+                device_id_type=pl.DeviceIdType.MESH,
+            )
+
+    def greeted(self):
+        pl.semaphore_wait(pltpu.get_barrier_semaphore(), 34)
+
+
+class Projection:
+    def __init__(self, here, refs, weight, wide, transposed):
+        self.here = here
+        self.weight = weight
+        self.wide = wide
+        self.transposed = transposed
+        (
+            self.mine,
+            self.spread,
+            self.rows,
+            self.partial,
+            self.relay,
+            self.last,
+            self.ready,
+            self.owned,
+            self.zsem,
+            self.gsem,
+            self.csem,
+            self.rsem,
+            self.osem,
+        ) = refs
+        self.sent = []
+
+    @staticmethod
+    def scratch(wide, kind):
+        return [
+            pltpu.VMEM((4, 8, DEPTH), jnp.bfloat16),
+            pltpu.VMEM((4, 8, DEPTH), jnp.bfloat16),
+            pltpu.VMEM((1024, DEPTH), jnp.bfloat16),
+            pltpu.VMEM((4, 4, 64, wide), kind),
+            pltpu.VMEM((4, 2, 32, wide), kind),
+            pltpu.VMEM((4, 2, 64, wide), kind),
+            pltpu.VMEM((4, 8, 8, wide), jnp.bfloat16),
+            pltpu.VMEM((32, 8, wide), jnp.bfloat16),
+            pltpu.SemaphoreType.DMA((2, 4)),
+            pltpu.SemaphoreType.DMA((2, 128)),
+            pltpu.SemaphoreType.DMA((2, 32)),
+            pltpu.SemaphoreType.DMA((2, 16)),
+            pltpu.SemaphoreType.DMA((2, 32)),
+        ]
+
+    def push(self, *args):
+        copy = remote(*args)
+        copy.start()
+        self.sent.append(copy)
+
+    def exchange(self):
+        z = self.here.z
+        for dz in (1, 3, 2):
+            to = (z + dz) % 4
+            self.push(
+                self.mine.at[to],
+                self.spread.at[z],
+                self.zsem.at[0, dz],
+                self.zsem.at[1, dz],
+                self.here.device(dz=dz),
+            )
+        self.spread[z] = self.mine[z]
+
+    def exchanged(self):
+        z = self.here.z
+        for dz in (1, 3, 2):
+            slot = self.spread.at[(z + 4 - dz) % 4]
+            remote(
+                slot, slot, self.zsem.at[0, dz], self.zsem.at[1, dz], self.here.device(dz=1)
+            ).wait_recv()
+        for part in range(2):
+            both = jnp.concatenate([self.spread[2 * part], self.spread[2 * part + 1]], axis=0)
+            self.rows[pl.ds(self.start_of(part, 0, 0, 0), 16), :] = both
+
+    def start_of(self, part, u, r, core):
+        w, i = PLACE[(u, r)]
+        return w * 256 + part * 128 + (i * 2 + core) * 16
+
+    def slot(self, part, u, r, core, half=None):
+        columns = pl.ds(0, DEPTH) if half is None else pl.ds(half * (DEPTH // 2), DEPTH // 2)
+        return self.rows.at[pl.ds(self.start_of(part, u, r, core), 16), columns]
+
+    def gather_sem(self, side, part, u, r, half):
+        return self.gsem.at[side, ((part * 4 + u) * 4 + r) * 2 + (half or 0)]
+
+    def along(self, part, first, step):
+        if first == (part == 0):
+            return self.here.device(dx=step)
+        return self.here.device(dy=step)
+
+    def hop(self, part, u, r, first, step, half=None):
+        nu, nr = (u, (r - step) % 4) if first else ((u - step) % 4, r)
+        self.push(
+            self.slot(part, u, r, 0, half),
+            self.slot(part, nu, nr, 0, half),
+            self.gather_sem(0, part, nu, nr, half),
+            self.gather_sem(1, part, nu, nr, half),
+            self.along(part, first, step),
+        )
+
+    def to_sibling(self, part, u, r):
+        k = (part * 4 + u) * 4 + r
+        self.push(
+            self.slot(part, u, r, 0),
+            self.slot(part, u, r, 1),
+            self.csem.at[0, k],
+            self.csem.at[1, k],
+            self.here.device(dc=1),
+        )
+
+    def arrived(self, part, u, r):
+        halves = (0, 1) if (u == 2 or (u == 0 and r == 2)) else (None,)
+        for half in halves:
+            slot = self.slot(part, u, r, 0, half)
+            remote(
+                slot,
+                slot,
+                self.gather_sem(0, part, u, r, half),
+                self.gather_sem(1, part, u, r, half),
+                self.here.device(dc=1),
+            ).wait_recv()
+
+    def sibling_arrived(self, part, u, r):
+        k = (part * 4 + u) * 4 + r
+        slot = self.slot(part, u, r, 1)
+        remote(
+            slot, slot, self.csem.at[0, k], self.csem.at[1, k], self.here.device(dc=1)
+        ).wait_recv()
+
+    def second(self, part, r):
+        self.hop(part, 0, r, False, 1)
+        self.hop(part, 0, r, False, -1)
+        self.to_sibling(part, 0, r)
+
+    def first_ring(self):
+        for part in range(2):
+            self.hop(part, 0, 0, True, 1)
+            self.hop(part, 0, 0, True, -1)
+        for part in range(2):
+            self.second(part, 0)
+        for r, step in ((3, 1), (1, -1)):
+            for part in range(2):
+                self.arrived(part, 0, r)
+                self.hop(part, 0, r, True, step, 0 if step == 1 else 1)
+                self.second(part, r)
+        for part in range(2):
+            self.arrived(part, 0, 2)
+            self.second(part, 2)
+
+    def second_ring(self, r):
+        for u, step in ((3, 1), (1, -1)):
+            for part in range(2):
+                self.arrived(part, u, r)
+                self.hop(part, u, r, False, step, 0 if step == 1 else 1)
+                self.to_sibling(part, u, r)
+
+    def last_ring(self):
+        for r in (0, 3, 1, 2):
+            for part in range(2):
+                self.arrived(part, 2, r)
+                self.to_sibling(part, 2, r)
+
+    def dots(self, w):
+        for u, r in UNITS[w]:
+            for part in range(2):
+                self.sibling_arrived(part, u, r)
+
+        def tile(start, width):
+            lhs = self.rows[pl.ds(w * 256, 256), :]
+            if self.transposed:
+                out = lax.dot_general(
+                    lhs,
+                    self.weight[pl.ds(start, width), :],
+                    (((1,), (1,)), ((), ())),
+                    preferred_element_type=jnp.float32,
+                )
+            else:
+                out = jnp.dot(
+                    lhs,
+                    self.weight[:, pl.ds(start, width)],
+                    preferred_element_type=jnp.float32,
+                )
+            out = out.reshape(2, 8, 2, 8, width)
+            for d in range(4):
+                self.partial[w, d, :, pl.ds(start, width)] = (
+                    out[d // 2, :, d % 2].reshape(64, width).astype(self.partial.dtype)
+                )
+
+        @pl.loop(0, self.wide // 256)
+        def _(n):
+            tile(pl.multiple_of(n * 256, 256), 256)
+
+        if self.wide % 256:
+            tile(self.wide // 256 * 256, self.wide % 256)
+
+    def ring_copy(self, src, dst, k, dz):
+        self.push(src, dst, self.rsem.at[0, k], self.rsem.at[1, k], self.here.device(dz=dz))
+
+    def ring_wait(self, dst, k):
+        remote(
+            dst, dst, self.rsem.at[0, k], self.rsem.at[1, k], self.here.device(dz=1)
+        ).wait_recv()
+
+    def relay_out(self, w):
+        far = (self.here.z + 2) % 4
+        self.ring_copy(self.partial.at[w, far, pl.ds(0, 32)], self.relay.at[w, 0], w * 4, 1)
+        self.ring_copy(self.partial.at[w, far, pl.ds(32, 32)], self.relay.at[w, 1], w * 4 + 1, -1)
+
+    def neighbours_out(self, w):
+        for side, dz in ((0, 1), (1, -1)):
+            to = (self.here.z + dz) % 4
+            half = pl.ds(32 * side, 32)
+            self.ring_wait(self.relay.at[w, side], w * 4 + side)
+            total = self.partial[w, to, half, :].astype(jnp.float32) + self.relay[w, side].astype(
+                jnp.float32
+            )
+            self.partial[w, to, half, :] = total.astype(self.partial.dtype)
+            self.ring_copy(self.partial.at[w, to], self.last.at[w, side], w * 4 + 2 + side, dz)
+
+    def owners_out(self, w):
+        here = self.here
+        total = self.partial[w, here.z].astype(jnp.float32)
+        for side in range(2):
+            self.ring_wait(self.last.at[w, side], w * 4 + 2 + side)
+            total = total + self.last[w, side].astype(jnp.float32)
+        self.ready[w] = total.reshape(8, 8, self.wide).astype(jnp.bfloat16)
+        for i, (u, r) in enumerate(UNITS[w]):
+            for core in range(2):
+                j = i * 2 + core
+                if w == 0 and j == 0:
+                    self.owned[here.gx] = self.ready[0, 0]
+                    continue
+                self.push(
+                    self.ready.at[w, j],
+                    self.owned.at[here.gx],
+                    self.osem.at[0, w * 8 + j],
+                    self.osem.at[1, w * 8 + j],
+                    self.owner(u, r, core),
+                )
+
+    def owner(self, u, r, core):
+        first = self.here.z < 2
+        dy = jnp.where(first, u, r)
+        dx = jnp.where(first, r, u)
+        return self.here.device(dy, dx, core)
+
+    def owners_in(self):
+        for w in range(4):
+            for i, (u, r) in enumerate(UNITS[w]):
+                for core in range(2):
+                    j = i * 2 + core
+                    if w == 0 and j == 0:
+                        continue
+                    source, _ = self.owner(4 - u, 4 - r, core)
+                    slot = self.owned.at[source]
+                    remote(
+                        slot,
+                        slot,
+                        self.osem.at[0, w * 8 + j],
+                        self.osem.at[1, w * 8 + j],
+                        self.here.device(dc=1),
+                    ).wait_recv()
+
+    def run(self, weight_in):
+        self.exchanged()
+        self.first_ring()
+        weight_in()
+        self.dots(0)
+        self.relay_out(0)
+        self.second_ring(0)
+        self.second_ring(3)
+        self.neighbours_out(0)
+        self.dots(1)
+        self.relay_out(1)
+        self.second_ring(1)
+        self.second_ring(2)
+        self.neighbours_out(1)
+        self.dots(2)
+        self.relay_out(2)
+        self.owners_out(0)
+        self.last_ring()
+        self.neighbours_out(2)
+        self.dots(3)
+        self.relay_out(3)
+        self.owners_out(1)
+        self.neighbours_out(3)
+        self.owners_out(2)
+        self.owners_out(3)
+        self.owners_in()
+
+    def finish(self):
+        for copy in self.sent:
+            copy.wait_send()
+
+
+def project_in(hidden, gain, w_t, out, weight, wsem, *refs):
+    here = Here()
+    here.greet()
+    load = pltpu.make_async_copy(
+        w_t, weight.at[pl.ds(pl.multiple_of(here.c * 64, 64), 576), :], wsem
+    )
+    load.start()
+    weight[pl.ds(pl.multiple_of((1 - here.c) * 576, 64), 64), :] = jnp.zeros(
+        (64, DEPTH), jnp.bfloat16
+    )
+    step = Projection(here, refs, weight, QWIDE, True)
+    widened = hidden[...].astype(jnp.float32)
+    scale = lax.rsqrt(jnp.mean(widened * widened, axis=-1, keepdims=True) + eps)
+    for z in range(4):
+        columns = pl.ds(z * DEPTH, DEPTH)
+        step.mine[z] = (hidden[:, columns].astype(jnp.float32) * scale * gain[:, columns]).astype(
+            jnp.bfloat16
+        )
+    here.greeted()
+    step.exchange()
+    step.run(load.wait)
+    out[...] = step.owned[...]
+    step.finish()
+
+
+def project_out(attended, w, out, weight, wsem, *refs):
+    here = Here()
+    here.greet()
+    load = pltpu.make_async_copy(w, weight, wsem)
+    load.start()
+    step = Projection(here, refs, weight, 512, False)
+    for z in range(4):
+        step.mine[z] = attended[:, pl.ds(z * DEPTH, DEPTH)]
+    here.greeted()
+    step.exchange()
+    step.run(load.wait)
+    for g in range(32):
+        out[:, pl.ds(g * 512, 512)] = step.owned[g]
+    step.finish()
+
+
+def vmem():
+    return pl.BlockSpec(memory_space=pltpu.VMEM)
+
+
+def hbm():
+    return pl.BlockSpec(memory_space=pl.ANY)
+
+
+def call_in(hidden, gain, w_t):
+    return pl.pallas_call(
+        project_in,
+        out_shape=jax.ShapeDtypeStruct((32, 8, QWIDE), jnp.bfloat16),
+        in_specs=[vmem(), vmem(), hbm()],
+        out_specs=vmem(),
+        scratch_shapes=[pltpu.VMEM((QWIDE, DEPTH), jnp.bfloat16), pltpu.SemaphoreType.DMA]
+        + Projection.scratch(QWIDE, jnp.float32),
+        compiler_params=pltpu.CompilerParams(
+            collective_id=0, has_side_effects=True, vmem_limit_bytes=56 * 1024 * 1024
+        ),
+        name="project_in",
+    )(hidden, gain.reshape(1, -1), w_t)
+
+
+def call_out(attended, w):
+    return pl.pallas_call(
+        project_out,
+        out_shape=jax.ShapeDtypeStruct((8, 16384), jnp.bfloat16),
+        in_specs=[vmem(), hbm()],
+        out_specs=vmem(),
+        scratch_shapes=[pltpu.VMEM((DEPTH, 512), jnp.bfloat16), pltpu.SemaphoreType.DMA]
+        + Projection.scratch(512, jnp.bfloat16),
+        compiler_params=pltpu.CompilerParams(
+            collective_id=1, has_side_effects=True, vmem_limit_bytes=56 * 1024 * 1024
+        ),
+        name="project_out",
+    )(attended, w)
 
 
 def rotate(values, position, head_size):
@@ -64,33 +496,12 @@
 
 
 def on_device(hidden_in, norm_gain, w_qkv, k_cache, v_cache, lengths, w_out):
-    widened = hidden_in.astype(jnp.float32)
-    normed = (
-        widened * lax.rsqrt(jnp.mean(widened * widened, axis=-1, keepdims=True) + eps) * norm_gain
-    ).astype(jnp.bfloat16)
-    grouped_in = lax.all_gather(normed, "gx", axis=0, tiled=True)
-    spread_in = lax.all_to_all(grouped_in, "gy", split_axis=1, concat_axis=0, tiled=True)
-    picked = spread_in
-    partial_qkv = lax.psum_scatter(
-        jnp.dot(picked, w_qkv, preferred_element_type=jnp.float32),
-        "gy",
-        scatter_dimension=0,
-        tiled=True,
-    )
-    owned = lax.all_to_all(
-        partial_qkv.astype(jnp.bfloat16), "gx", split_axis=0, concat_axis=1, tiled=True
-    )
+    blocks = call_in(hidden_in, norm_gain, w_qkv.T)
+    pairs = blocks.reshape(16, 2, 8, QWIDE)
+    joined = jnp.concatenate([pairs[:, 0, :, :576], pairs[:, 1, :, 64:]], axis=-1)
+    owned = joined.transpose(1, 0, 2).reshape(8, 18432)
     attended = attend_local(owned, k_cache, v_cache, lengths)
-    grouped_out = lax.all_gather(attended, "gx", axis=0, tiled=True)
-    spread_out = lax.all_to_all(grouped_out, "gy", split_axis=1, concat_axis=0, tiled=True)
-    picked = spread_out
-    partial_out = lax.psum_scatter(
-        jnp.dot(picked, w_out, preferred_element_type=jnp.float32).astype(jnp.bfloat16),
-        "gy",
-        scatter_dimension=0,
-        tiled=True,
-    )
-    return lax.all_to_all(partial_out, "gx", split_axis=0, concat_axis=1, tiled=True)
+    return call_out(attended, w_out)
 
 
 def solution(mesh):

time: 492 us -> 148 us (0.30)
  blocking collectives: 220 us -> 0 us
  waiting for transfers between devices: 166 us -> 0 us
  Pallas kernels: 0 us -> 132 us
  local copies, waits for them, and re-layouts: 49.6 us -> 3.78 us
  matrix products: 29.1 us -> 8.53 us
  between operations: 13.3 us -> 0.15 us
  starting transfers between devices: 7.61 us -> 0 us
    all_to_all x3 -> x0, blocking collectives: 220 us -> none  [the longest x1 101 us: on_device(): lax.all_to_all(grouped_in, 'gy', split_axis=1, concat_axis=0, tiled=True)]
    pallas_call x0 -> x2, Pallas kernels: none -> 132 us  [the longest x1 72.6 us: call_in(): pl.pallas_call(project_in, out_shape=jax.ShapeDtypeStruct((32, 8, QWIDE),...]
    all_gather x2 -> x0, waiting for transfers between devices: 106 us -> none  [the longest x1 56.5 us: on_device(): grouped_in = lax.all_gather(normed, 'gx', axis=0, tiled=True)]
    reduce_scatter x2 -> x0, waiting for transfers between devices: 50.5 us -> none  [the longest x1 30.3 us: on_device(): lax.psum_scatter(jnp.dot(picked, w_qkv, preferred_element_type=jnp.float3...]
    all_gather x2 -> x0, local copies, waits for them, and re-layouts: 23.9 us -> none  [the longest x1 12 us: on_device(): grouped_in = lax.all_gather(normed, 'gx', axis=0, tiled=True)]
    all_to_all x4 -> x0, local copies, waits for them, and re-layouts: 23 us -> none  [the longest x1 11.3 us: on_device(): lax.all_to_all(grouped_in, 'gy', split_axis=1, concat_axis=0, tiled=True)]
    dot_general x2 -> x0, matrix products: 20.5 us -> none  [the longest x1 10.4 us: on_device(): jnp.dot(picked, w_qkv, preferred_element_type=jnp.float32)]
    all_to_all x1 -> x0, waiting for transfers between devices: 9.36 us -> none  [on_device(): lax.all_to_all(partial_qkv.astype(jnp.bfloat16), 'gx', split_axis=0, conc...]
  transfers between devices with their start and end apart: 5 -> 0, of which waited for: 5 -> 0; matrix products, arithmetic and copies ran while one was open for 0% -> 0% of each run, Pallas kernels for 0% -> 0%
where the time goes in v2:
time: 148 us; the launch traced here: 147 us
  Pallas kernels  132 us (89%)
  matrix products  8.53 us (6%)
  local copies, waits for them, and re-layouts  3.78 us (3%)
  other arithmetic  2.74 us (2%)
    pallas_call x1, Pallas kernels, call_in(): pl.pallas_call(project_in, out_shape=jax.ShapeDtypeStruct((32, 8, QWIDE),...  72.6 us
    pallas_call x1, Pallas kernels, call_out(): pl.pallas_call(project_out, out_shape=jax.ShapeDtypeStruct((8, 16384), jn...  59.6 us
    dot_general x1, matrix products, attend_local(): jnp.einsum('rgsd,rtgd->rgst', grouped, keys, preferred_element_type=jnp.f...  6.06 us

profile of v2, /device:TPU:1, one launch (start us, length us, event | category | flops | bytes accessed | tf_op | source)
XLA Modules:
  0.0 147.3 jit_solution(1607935219462987066)
XLA Ops:
  0.0 0.7 convert_element_type.44
  0.7 0.7 iota_compare_fusion
  1.4 0.1 multiply_cosine_fusion
  1.5 72.6 %project_in.1 = bf16[32,8,640]{2,1,0:T(8,128)(2,1)} custom-call(bf16[8,16384]{1,0:T(8,128)(2,1)} %hidden.1, f32[1,16384]{1,0:T(1,128)} %bitcast.71, bf16[576,4096]{1,0:T(8,128)(2,1)} %bitcast.59), custom_call_target="tpu_custom_call" | custom-call | tf_op jit(solution)/shard_map/project_in/pallas_call | solution.py:420
  74.1 1.1 slice_bitcast_fusion.1
  75.2 0.1 pad_maximum_fusion
  75.3 0.1 subtract_convert_fusion.1
  75.4 0.1 maximum_bitcast_fusion
  75.6 0.1 copy.38
  75.7 0.0 slice-start
  75.7 0.2 subtract_convert_fusion
  75.9 0.3 fusion.19
  76.2 0.0 slice-start.1
  76.3 6.1 %fusion.6 = (f32[8,8,16]{2,1,0:T(8,128)S(1)}, f32[8,8,16,512]{3,2,1,0:T(8,128)S(1)}) fusion(pred[8,512]{1,0:T(8,128)(4,1)S(1)} %iota_compare_fusion, bf16[8,8,16,64]{3,2,1,0:T(8,128)(2,1)S(1)} %bitcast.67, bf16[8,8,16,64]{3,2,1,0:T(8,128)(2,1)S(1)} %bitcast.65, bf16[8,512,1024]{2,1,0:T(8,128)(2,1)} %param.10), kind=kOutput, calls=%fused_computation.9 | convolution fusion | flops 136313856 | bytes 10756096 | tf_op jit(solution)/shard_map/rgsd,rtgd->rgst/dot_general | solution.py:488
  82.3 0.6 fusion.7
  83.0 0.0 slice-done
  83.0 0.0 slice-done.1
  83.1 2.1 %fusion.11 = bf16[8,8,16,128]{3,2,1,0:T(8,128)(2,1)S(1)} fusion(f32[8,8,16,512]{3,2,1,0:T(8,128)S(1)} %get-tuple-element.18, f32[8,8,16]{2,1,0:T(8,128)S(1)} %get-tuple-element.12, f32[8,8,16]{2,1,0:T(8,128)S(1)} %multiply_maximum_fusion, pred[8,512]{1,0:T(8,128)(4,1)S(1)} %iota_compare_fusion, f32[8,8,128]{2,1,0:T(8,128)S(1)} %bitcast.72, ...), kind=kOutput, calls=%fused_computation.12 | convolution fusion | flops 137232384 | bytes 10797056 | tf_op jit(solution)/shard_map/rgst,rtgd->rgsd/dot_general | solution.py:493
  85.2 0.9 copy.39
  86.1 59.6 %project_out.1 = bf16[8,16384]{1,0:T(8,128)(2,1)} custom-call(bf16[8,16384]{1,0:T(8,128)(2,1)} %bitcast.63, bf16[4096,512]{1,0:T(8,128)(2,1)} %w.1), custom_call_target="tpu_custom_call" | custom-call | tf_op jit(solution)/shard_map/project_out/pallas_call | solution.py:435
  145.7 1.7 %copy.42 = bf16[8,16384]{1,0:T(8,128)(2,1)} copy(bf16[8,16384]{1,0:T(8,128)(2,1)} %project_out.1) | data formatting | bytes 524288
  (7 shorter events, 0.1 us)
Async XLA Ops:
  75.7 7.4 %slice-start = ((s8[8388608]{0:T(1024)(128)(4,1)}), s8[4194304]{0:T(1024)(128)(4,1)S(1)}, s32[]{:S(2)}) async-start(s8[8388608]{0:T(1024)(128)(4,1)} %bitcast.73), calls=%async_computation | async-start | bytes 8388608
  76.2 6.8 %slice-start.1 = ((s8[8388608]{0:T(1024)(128)(4,1)}), s8[4194304]{0:T(1024)(128)(4,1)S(1)}, s32[]{:S(2)}) async-start(s8[8388608]{0:T(1024)(128)(4,1)} %bitcast.73), calls=%async_computation.1 | async-start | bytes 8388608

commit v3 on v2

--- a/solution.py
+++ b/solution.py
@@ -1,4 +1,3 @@
-import functools
 import math
 
 import jax
@@ -11,6 +10,8 @@
 HQ = 128
 KVH = 8
 HD = 128
+ROWS = 8
+CACHE = 512
 DEPTH = 4096
 QWIDE = 640
 
@@ -367,17 +368,7 @@
             copy.wait_send()
 
 
-def project_in(hidden, gain, w_t, out, weight, wsem, *refs):
-    here = Here()
-    here.greet()
-    load = pltpu.make_async_copy(
-        w_t, weight.at[pl.ds(pl.multiple_of(here.c * 64, 64), 576), :], wsem
-    )
-    load.start()
-    weight[pl.ds(pl.multiple_of((1 - here.c) * 576, 64), 64), :] = jnp.zeros(
-        (64, DEPTH), jnp.bfloat16
-    )
-    step = Projection(here, refs, weight, QWIDE, True)
+def normalized(step, hidden, gain):
     widened = hidden[...].astype(jnp.float32)
     scale = lax.rsqrt(jnp.mean(widened * widened, axis=-1, keepdims=True) + eps)
     for z in range(4):
@@ -385,123 +376,162 @@
         step.mine[z] = (hidden[:, columns].astype(jnp.float32) * scale * gain[:, columns]).astype(
             jnp.bfloat16
         )
-    here.greeted()
-    step.exchange()
-    step.run(load.wait)
-    out[...] = step.owned[...]
-    step.finish()
-
-
-def project_out(attended, w, out, weight, wsem, *refs):
+
+
+def turn(lengths, freqs, turns):
+    row = lax.broadcasted_iota(jnp.int32, (ROWS, HD), 0)
+    lane = lax.broadcasted_iota(jnp.int32, (ROWS, HD), 1)
+    position = jnp.zeros((ROWS, HD), jnp.float32)
+    for r in range(ROWS):
+        position = jnp.where(row == r, lengths[r].astype(jnp.float32), position)
+    angle = position * freqs[...]
+    turns[0] = jnp.cos(angle)
+    turns[1] = jnp.where(lane < HD // 2, -jnp.sin(angle), jnp.sin(angle))
+
+
+def heads(owned, turns, qkv):
+    lane = lax.broadcasted_iota(jnp.int32, (ROWS, HD), 1)
+    for pair in range(16):
+        even = owned[2 * pair].astype(jnp.float32)
+        odd = owned[2 * pair + 1].astype(jnp.float32)
+        for t in range(9):
+            if t < 4:
+                head = even[:, t * HD : (t + 1) * HD]
+            elif t > 4:
+                head = odd[:, (t - 4) * HD : (t - 3) * HD]
+            else:
+                head = jnp.where(lane < HD // 2, even[:, 4 * HD :], odd[:, :HD])
+            h = pair * 9 + t
+            if h < HQ + KVH:
+                head = head * turns[0] + pltpu.roll(head, HD // 2, 1) * turns[1]
+                head = head.astype(jnp.bfloat16).astype(jnp.float32)
+            qkv[pl.ds(h * ROWS, ROWS), :] = head
+
+
+def attend(lengths, keys, values, qkv, mixed, out):
+    share = HQ // KVH
+    scale = 1.0 / math.sqrt(HD)
+
+    @pl.loop(0, ROWS)
+    def _(r):
+        valid = lax.broadcasted_iota(jnp.int32, (share, CACHE), 1) < lengths[r]
+        for g in range(KVH):
+            columns = pl.ds(g * HD, HD)
+            span = pl.ds(g * share * ROWS + r, share, stride=ROWS)
+            query = qkv[span, :]
+            key_new = qkv[pl.ds((HQ + g) * ROWS + r, 1), :]
+            value_new = qkv[pl.ds((HQ + KVH + g) * ROWS + r, 1), :]
+            fresh = jnp.sum(query * key_new, axis=1, keepdims=True) * scale
+            scores = (
+                lax.dot_general(
+                    query.astype(jnp.bfloat16),
+                    keys[r, :, columns],
+                    (((1,), (1,)), ((), ())),
+                    preferred_element_type=jnp.float32,
+                )
+                * scale
+            )
+            scores = jnp.where(valid, scores, -jnp.inf)
+            top = jnp.maximum(jnp.max(scores, axis=1, keepdims=True), fresh)
+            probs = jnp.exp(scores - top)
+            pnew = jnp.exp(fresh - top)
+            total = jnp.sum(probs, axis=1, keepdims=True) + pnew
+            weights = (probs / total).astype(jnp.bfloat16)
+            wnew = (pnew / total).astype(jnp.bfloat16).astype(jnp.float32)
+            mixed[span, :] = (
+                jnp.dot(weights, values[r, :, columns], preferred_element_type=jnp.float32)
+                + wnew * value_new
+            )
+
+    for h in range(HQ):
+        out[h // 32, :, pl.ds(h % 32 * HD, HD)] = mixed[pl.ds(h * ROWS, ROWS), :].astype(
+            jnp.bfloat16
+        )
+
+
+def layer(
+    lengths,
+    hidden,
+    gain,
+    freqs,
+    w_qkv,
+    k_cache,
+    v_cache,
+    w_out,
+    out,
+    weight_in,
+    keys,
+    values,
+    weight_out,
+    turns,
+    qkv,
+    mixed,
+    loads,
+    *refs,
+):
     here = Here()
     here.greet()
-    load = pltpu.make_async_copy(w, weight, wsem)
-    load.start()
-    step = Projection(here, refs, weight, 512, False)
-    for z in range(4):
-        step.mine[z] = attended[:, pl.ds(z * DEPTH, DEPTH)]
+    count = len(refs) // 2
+    first = Projection(here, refs[:count], weight_in, QWIDE, True)
+    second = Projection(here, refs[count:], weight_out, 512, False)
+    fetch = [
+        pltpu.make_async_copy(
+            w_qkv, weight_in.at[pl.ds(pl.multiple_of(here.c * 64, 64), 576), :], loads.at[0]
+        ),
+        pltpu.make_async_copy(k_cache, keys, loads.at[1]),
+        pltpu.make_async_copy(v_cache, values, loads.at[2]),
+        pltpu.make_async_copy(w_out, weight_out, loads.at[3]),
+    ]
+    for copy in fetch:
+        copy.start()
+    weight_in[pl.ds(pl.multiple_of((1 - here.c) * 576, 64), 64), :] = jnp.zeros(
+        (64, DEPTH), jnp.bfloat16
+    )
+    normalized(first, hidden, gain)
     here.greeted()
-    step.exchange()
-    step.run(load.wait)
-    for g in range(32):
-        out[:, pl.ds(g * 512, 512)] = step.owned[g]
-    step.finish()
-
-
-def vmem():
-    return pl.BlockSpec(memory_space=pltpu.VMEM)
-
-
-def hbm():
-    return pl.BlockSpec(memory_space=pl.ANY)
-
-
-def call_in(hidden, gain, w_t):
-    return pl.pallas_call(
-        project_in,
-        out_shape=jax.ShapeDtypeStruct((32, 8, QWIDE), jnp.bfloat16),
-        in_specs=[vmem(), vmem(), hbm()],
-        out_specs=vmem(),
-        scratch_shapes=[pltpu.VMEM((QWIDE, DEPTH), jnp.bfloat16), pltpu.SemaphoreType.DMA]
-        + Projection.scratch(QWIDE, jnp.float32),
-        compiler_params=pltpu.CompilerParams(
-            collective_id=0, has_side_effects=True, vmem_limit_bytes=56 * 1024 * 1024
-        ),
-        name="project_in",
-    )(hidden, gain.reshape(1, -1), w_t)
-
-
-def call_out(attended, w):
-    return pl.pallas_call(
-        project_out,
-        out_shape=jax.ShapeDtypeStruct((8, 16384), jnp.bfloat16),
-        in_specs=[vmem(), hbm()],
-        out_specs=vmem(),
-        scratch_shapes=[pltpu.VMEM((DEPTH, 512), jnp.bfloat16), pltpu.SemaphoreType.DMA]
+    first.exchange()
+    turn(lengths, freqs, turns)
+    first.run(fetch[0].wait)
+    heads(first.owned, turns, qkv)
+    fetch[1].wait()
+    fetch[2].wait()
+    attend(lengths, keys, values, qkv, mixed, second.mine)
+    second.exchange()
+    second.run(fetch[3].wait)
+    out[...] = second.owned[...]
+    first.finish()
+    second.finish()
+
+
+def on_device(hidden_in, norm_gain, w_qkv, k_cache, v_cache, lengths, w_out):
+    half = jnp.arange(HD // 2, dtype=jnp.float32)
+    freqs = theta ** (-2.0 * half / HD)
+    freqs = jnp.concatenate([freqs, freqs]).reshape(1, HD)
+    vmem = pl.BlockSpec(memory_space=pltpu.VMEM)
+    hbm = pl.BlockSpec(memory_space=pl.ANY)
+    blocks = pl.pallas_call(
+        layer,
+        out_shape=jax.ShapeDtypeStruct((32, ROWS, 512), jnp.bfloat16),
+        in_specs=[pl.BlockSpec(memory_space=pltpu.SMEM), vmem, vmem, vmem, hbm, hbm, hbm, hbm],
+        out_specs=vmem,
+        scratch_shapes=[
+            pltpu.VMEM((QWIDE, DEPTH), jnp.bfloat16),
+            pltpu.VMEM((ROWS, CACHE, KVH * HD), jnp.bfloat16),
+            pltpu.VMEM((ROWS, CACHE, KVH * HD), jnp.bfloat16),
+            pltpu.VMEM((DEPTH, 512), jnp.bfloat16),
+            pltpu.VMEM((2, ROWS, HD), jnp.float32),
+            pltpu.VMEM(((HQ + 2 * KVH) * ROWS, HD), jnp.float32),
+            pltpu.VMEM((HQ * ROWS, HD), jnp.float32),
+            pltpu.SemaphoreType.DMA((4,)),
+        ]
+        + Projection.scratch(QWIDE, jnp.float32)
         + Projection.scratch(512, jnp.bfloat16),
         compiler_params=pltpu.CompilerParams(
-            collective_id=1, has_side_effects=True, vmem_limit_bytes=56 * 1024 * 1024
+            collective_id=0, has_side_effects=True, vmem_limit_bytes=60 * 1024 * 1024
         ),
-        name="project_out",
-    )(attended, w)
-
-
-def rotate(values, position, head_size):
-    half = head_size // 2
-    index = jnp.arange(half, dtype=jnp.float32)
-    freqs = theta ** (-2.0 * index / head_size)
-    angle = position[:, None, None] * freqs[None, None, :]
-    cosine = jnp.cos(angle)
-    sine = jnp.sin(angle)
-    first = values[..., :half]
-    second = values[..., half:]
-    return jnp.concatenate(
-        [first * cosine - second * sine, second * cosine + first * sine], axis=-1
-    )
-
-
-def normalize(scores, fresh):
-    top = jnp.maximum(jnp.max(scores, axis=-1), fresh)
-    probs = jnp.exp(scores - top[..., None])
-    pnew = jnp.exp(fresh - top)
-    total = jnp.sum(probs, axis=-1) + pnew
-    return ((probs / total[..., None]).astype(jnp.bfloat16), (pnew / total).astype(jnp.bfloat16))
-
-
-def attend_local(owned, k_cache, v_cache, lengths):
-    rows = owned.shape[0]
-    span = k_cache.shape[1]
-    share = HQ // KVH
-    query = owned[:, : HQ * HD].reshape(rows, HQ, HD).astype(jnp.float32)
-    key_new = owned[:, HQ * HD : (HQ + KVH) * HD].reshape(rows, KVH, HD).astype(jnp.float32)
-    value_new = owned[:, (HQ + KVH) * HD :].reshape(rows, KVH, HD).astype(jnp.float32)
-    position = lengths.astype(jnp.float32)
-    grouped = rotate(query, position, HD).astype(jnp.bfloat16).reshape(rows, KVH, share, HD)
-    key_new = rotate(key_new, position, HD).astype(jnp.bfloat16)
-    keys = k_cache.reshape(rows, span, KVH, HD)
-    values = v_cache.reshape(rows, span, KVH, HD)
-    scale = 1.0 / math.sqrt(HD)
-    fresh = (
-        jnp.einsum("rgsd,rgd->rgs", grouped, key_new, preferred_element_type=jnp.float32) * scale
-    )
-    scores = (
-        jnp.einsum("rgsd,rtgd->rgst", grouped, keys, preferred_element_type=jnp.float32) * scale
-    )
-    valid = jnp.arange(span, dtype=jnp.int32)[None, :] < lengths[:, None]
-    scores = jnp.where(valid[:, None, None, :], scores, -jnp.inf)
-    weights, wnew = normalize(scores, fresh)
-    mixed = jnp.einsum("rgst,rtgd->rgsd", weights, values, preferred_element_type=jnp.float32)
-    mixed = mixed + wnew.astype(jnp.float32)[..., None] * value_new[:, :, None, :]
-    return mixed.reshape(rows, HQ * HD).astype(jnp.bfloat16)
-
-
-def on_device(hidden_in, norm_gain, w_qkv, k_cache, v_cache, lengths, w_out):
-    blocks = call_in(hidden_in, norm_gain, w_qkv.T)
-    pairs = blocks.reshape(16, 2, 8, QWIDE)
-    joined = jnp.concatenate([pairs[:, 0, :, :576], pairs[:, 1, :, 64:]], axis=-1)
-    owned = joined.transpose(1, 0, 2).reshape(8, 18432)
-    attended = attend_local(owned, k_cache, v_cache, lengths)
-    return call_out(attended, w_out)
+        name="layer",
+    )(lengths, hidden_in, norm_gain.reshape(1, -1), freqs, w_qkv.T, k_cache, v_cache, w_out)
+    return blocks.transpose(1, 0, 2).reshape(ROWS, 32 * 512)
 
 
 def solution(mesh):

time: 148 us -> 151 us (1.020)
  Pallas kernels: 132 us -> 149 us
  matrix products: 8.53 us -> 0 us
  other arithmetic: 2.74 us -> 0.6 us
  local copies, waits for them, and re-layouts: 3.78 us -> 1.67 us
    pallas_call x2 -> x1, Pallas kernels: 132 us -> 149 us  [on_device(): pl.pallas_call(layer, out_shape=jax.ShapeDtypeStruct((32, ROWS, 512), jnp...]
    dot_general x3 -> x0, matrix products: 8.53 us -> none  [the longest x1 6.06 us: attend_local(): jnp.einsum('rgsd,rtgd->rgst', grouped, keys, preferred_element_type=jnp.f...]
where the time goes in v3:
time: 151 us
  Pallas kernels  149 us (99%)
  local copies, waits for them, and re-layouts  1.67 us (1%)
    pallas_call x1, Pallas kernels, on_device(): pl.pallas_call(layer, out_shape=jax.ShapeDtypeStruct((32, ROWS, 512), jnp...  149 us

profile of v3, /device:TPU:1, one launch (start us, length us, event | category | flops | bytes accessed | tf_op | source)
XLA Modules:
  0.0 151.0 jit_solution(12975767072215629809)
XLA Ops:
  0.0 0.6 maximum_bitcast_fusion.freqs
  0.6 148.7 %layer.1 = bf16[32,8,512]{2,1,0:T(8,128)(2,1)} custom-call(s32[8]{0:T(128)} %lengths.1, bf16[8,16384]{1,0:T(8,128)(2,1)} %hidden.1, f32[1,16384]{1,0:T(1,128)} %bitcast.9, f32[1,128]{1,0:T(1,128)} %maximum_bitcast_fusion.freqs, bf16[576,4096]{1,0:T(8,128)(2,1)} %bitcast.7, bf16[8,512,1024]{2,1,0:T(8,128)(2,1)} %k_cache.1, bf16[8,512,1024]{2,1,0:T(8,128)(2,1)} %v_cache.1, ...), custom_call_target="tpu_custom_call" | custom-call | tf_op jit(solution)/shard_map/layer/pallas_call | solution.py:512
  149.3 1.7 %copy.9 = bf16[8,16384]{1,0:T(8,128)(2,1)} copy(bf16[8,16384]{1,0:T(8,128)(2,1)} %bitcast.8) | data formatting | bytes 524288
  (1 shorter events, 0.0 us)

commit v4 on v3

--- a/solution.py
+++ b/solution.py
@@ -19,11 +19,16 @@
 theta = 500000.0
 
 UNITS = (
-    ((0, 0), (0, 3), (0, 1), (0, 2)),
-    ((1, 0), (3, 0), (1, 3), (3, 3)),
-    ((1, 1), (3, 1), (1, 2), (3, 2)),
-    ((2, 0), (2, 3), (2, 1), (2, 2)),
+    ((0, 0), (0, 3)),
+    ((0, 1), (1, 0)),
+    ((3, 0), (0, 2)),
+    ((1, 3), (3, 3)),
+    ((1, 1), (3, 1)),
+    ((2, 0), (1, 2)),
+    ((3, 2), (2, 3)),
+    ((2, 1), (2, 2)),
 )
+DIRECT = (7,)
 PLACE = {ur: (w, i) for w, unit in enumerate(UNITS) for i, ur in enumerate(unit)}
 
 
@@ -55,26 +60,18 @@
 
     def greet(self):
         barrier = pltpu.get_barrier_semaphore()
-        for dy in range(4):
-            for dx in range(4):
-                for dc in range(2):
-                    if dy or dx or dc:
-                        pl.semaphore_signal(
-                            barrier,
-                            inc=1,
-                            device_id=self.device(dy, dx, dc),
-                            device_id_type=pl.DeviceIdType.MESH,
-                        )
-        for dz in range(1, 4):
+        partners = [dict(dz=1), dict(dz=3), dict(dz=2), dict(dc=1)]
+        partners += [dict(dx=1), dict(dx=3), dict(dy=1), dict(dy=3)]
+        for partner in partners:
             pl.semaphore_signal(
                 barrier,
                 inc=1,
-                device_id=self.device(dz=dz),
+                device_id=self.device(**partner),
                 device_id_type=pl.DeviceIdType.MESH,
             )
 
     def greeted(self):
-        pl.semaphore_wait(pltpu.get_barrier_semaphore(), 34)
+        pl.semaphore_wait(pltpu.get_barrier_semaphore(), 8)
 
 
 class Projection:
@@ -106,15 +103,15 @@
             pltpu.VMEM((4, 8, DEPTH), jnp.bfloat16),
             pltpu.VMEM((4, 8, DEPTH), jnp.bfloat16),
             pltpu.VMEM((1024, DEPTH), jnp.bfloat16),
-            pltpu.VMEM((4, 4, 64, wide), kind),
-            pltpu.VMEM((4, 2, 32, wide), kind),
-            pltpu.VMEM((4, 2, 64, wide), kind),
-            pltpu.VMEM((4, 8, 8, wide), jnp.bfloat16),
+            pltpu.VMEM((8, 4, 32, wide), kind),
+            pltpu.VMEM((8, 32, wide), kind),
+            pltpu.VMEM((8, 2, 32, wide), kind),
+            pltpu.VMEM((8, 4, 8, wide), jnp.bfloat16),
             pltpu.VMEM((32, 8, wide), jnp.bfloat16),
             pltpu.SemaphoreType.DMA((2, 4)),
             pltpu.SemaphoreType.DMA((2, 128)),
             pltpu.SemaphoreType.DMA((2, 32)),
-            pltpu.SemaphoreType.DMA((2, 16)),
+            pltpu.SemaphoreType.DMA((2, 32)),
             pltpu.SemaphoreType.DMA((2, 32)),
         ]
 
@@ -149,7 +146,7 @@
 
     def start_of(self, part, u, r, core):
         w, i = PLACE[(u, r)]
-        return w * 256 + part * 128 + (i * 2 + core) * 16
+        return w * 128 + part * 64 + (i * 2 + core) * 16
 
     def slot(self, part, u, r, core, half=None):
         columns = pl.ds(0, DEPTH) if half is None else pl.ds(half * (DEPTH // 2), DEPTH // 2)
@@ -202,38 +199,27 @@
             slot, slot, self.csem.at[0, k], self.csem.at[1, k], self.here.device(dc=1)
         ).wait_recv()
 
-    def second(self, part, r):
-        self.hop(part, 0, r, False, 1)
-        self.hop(part, 0, r, False, -1)
-        self.to_sibling(part, 0, r)
-
-    def first_ring(self):
+    def start(self):
+        for first in (True, False):
+            for part in range(2):
+                self.hop(part, 0, 0, first, 1)
+                self.hop(part, 0, 0, first, -1)
         for part in range(2):
-            self.hop(part, 0, 0, True, 1)
-            self.hop(part, 0, 0, True, -1)
+            self.to_sibling(part, 0, 0)
+
+    def second(self, r):
         for part in range(2):
-            self.second(part, 0)
-        for r, step in ((3, 1), (1, -1)):
-            for part in range(2):
-                self.arrived(part, 0, r)
-                self.hop(part, 0, r, True, step, 0 if step == 1 else 1)
-                self.second(part, r)
+            self.hop(part, 0, r, False, 1)
+            self.hop(part, 0, r, False, -1)
+
+    def take(self, u, r):
         for part in range(2):
-            self.arrived(part, 0, 2)
-            self.second(part, 2)
-
-    def second_ring(self, r):
-        for u, step in ((3, 1), (1, -1)):
-            for part in range(2):
-                self.arrived(part, u, r)
-                self.hop(part, u, r, False, step, 0 if step == 1 else 1)
-                self.to_sibling(part, u, r)
-
-    def last_ring(self):
-        for r in (0, 3, 1, 2):
-            for part in range(2):
-                self.arrived(part, 2, r)
-                self.to_sibling(part, 2, r)
+            self.arrived(part, u, r)
+            if u in (1, 3):
+                self.hop(part, u, r, False, 1 if u == 3 else -1, 0 if u == 3 else 1)
+            elif u == 0 and r in (1, 3):
+                self.hop(part, u, r, True, 1 if r == 3 else -1, 0 if r == 3 else 1)
+            self.to_sibling(part, u, r)
 
     def dots(self, w):
         for u, r in UNITS[w]:
@@ -241,7 +227,7 @@
                 self.sibling_arrived(part, u, r)
 
         def tile(start, width):
-            lhs = self.rows[pl.ds(w * 256, 256), :]
+            lhs = self.rows[pl.ds(w * 128, 128), :]
             if self.transposed:
                 out = lax.dot_general(
                     lhs,
@@ -255,10 +241,10 @@
                     self.weight[:, pl.ds(start, width)],
                     preferred_element_type=jnp.float32,
                 )
-            out = out.reshape(2, 8, 2, 8, width)
+            out = out.reshape(2, 4, 2, 8, width)
             for d in range(4):
                 self.partial[w, d, :, pl.ds(start, width)] = (
-                    out[d // 2, :, d % 2].reshape(64, width).astype(self.partial.dtype)
+                    out[d // 2, :, d % 2].reshape(32, width).astype(self.partial.dtype)
                 )
 
         @pl.loop(0, self.wide // 256)
@@ -277,18 +263,32 @@
         ).wait_recv()
 
     def relay_out(self, w):
-        far = (self.here.z + 2) % 4
-        self.ring_copy(self.partial.at[w, far, pl.ds(0, 32)], self.relay.at[w, 0], w * 4, 1)
-        self.ring_copy(self.partial.at[w, far, pl.ds(32, 32)], self.relay.at[w, 1], w * 4 + 1, -1)
+        z = self.here.z
+        far = (z + 2) % 4
+        if w in DIRECT:
+            for side, dz in ((0, 1), (1, -1)):
+                to = (z + dz) % 4
+                self.ring_copy(self.partial.at[w, to], self.last.at[w, side], w * 4 + 2 + side, dz)
+            self.ring_copy(self.partial.at[w, far], self.relay.at[w], w * 4, 2)
+            return
+        for side, dz in ((0, 1), (1, -1)):
+            self.ring_copy(
+                self.partial.at[w, far, pl.ds(16 * side, 16)],
+                self.relay.at[w, pl.ds(16 * side, 16)],
+                w * 4 + side,
+                dz,
+            )
 
     def neighbours_out(self, w):
+        if w in DIRECT:
+            return
         for side, dz in ((0, 1), (1, -1)):
             to = (self.here.z + dz) % 4
-            half = pl.ds(32 * side, 32)
-            self.ring_wait(self.relay.at[w, side], w * 4 + side)
-            total = self.partial[w, to, half, :].astype(jnp.float32) + self.relay[w, side].astype(
-                jnp.float32
-            )
+            half = pl.ds(16 * side, 16)
+            self.ring_wait(self.relay.at[w, half], w * 4 + side)
+            total = self.partial[w, to, half, :].astype(jnp.float32) + self.relay[
+                w, half, :
+            ].astype(jnp.float32)
             self.partial[w, to, half, :] = total.astype(self.partial.dtype)
             self.ring_copy(self.partial.at[w, to], self.last.at[w, side], w * 4 + 2 + side, dz)
 
@@ -298,7 +298,10 @@
         for side in range(2):
             self.ring_wait(self.last.at[w, side], w * 4 + 2 + side)
             total = total + self.last[w, side].astype(jnp.float32)
-        self.ready[w] = total.reshape(8, 8, self.wide).astype(jnp.bfloat16)
+        if w in DIRECT:
+            self.ring_wait(self.relay.at[w], w * 4)
+            total = total + self.relay[w].astype(jnp.float32)
+        self.ready[w] = total.reshape(4, 8, self.wide).astype(jnp.bfloat16)
         for i, (u, r) in enumerate(UNITS[w]):
             for core in range(2):
                 j = i * 2 + core
@@ -308,8 +311,8 @@
                 self.push(
                     self.ready.at[w, j],
                     self.owned.at[here.gx],
-                    self.osem.at[0, w * 8 + j],
-                    self.osem.at[1, w * 8 + j],
+                    self.osem.at[0, w * 4 + j],
+                    self.osem.at[1, w * 4 + j],
                     self.owner(u, r, core),
                 )
 
@@ -320,7 +323,7 @@
         return self.here.device(dy, dx, core)
 
     def owners_in(self):
-        for w in range(4):
+        for w in range(8):
             for i, (u, r) in enumerate(UNITS[w]):
                 for core in range(2):
                     j = i * 2 + core
@@ -331,37 +334,61 @@
                     remote(
                         slot,
                         slot,
-                        self.osem.at[0, w * 8 + j],
-                        self.osem.at[1, w * 8 + j],
+                        self.osem.at[0, w * 4 + j],
+                        self.osem.at[1, w * 4 + j],
                         self.here.device(dc=1),
                     ).wait_recv()
 
     def run(self, weight_in):
         self.exchanged()
-        self.first_ring()
+        self.start()
+        self.take(0, 3)
+        self.take(0, 1)
+        self.second(3)
+        self.second(1)
         weight_in()
-        self.dots(0)
-        self.relay_out(0)
-        self.second_ring(0)
-        self.second_ring(3)
+        self.unit(0)
+        self.take(3, 0)
+        self.take(1, 0)
+        self.unit(1)
+        self.take(0, 2)
+        self.second(2)
         self.neighbours_out(0)
-        self.dots(1)
-        self.relay_out(1)
-        self.second_ring(1)
-        self.second_ring(2)
+        self.unit(2)
+        self.take(3, 3)
+        self.take(1, 3)
         self.neighbours_out(1)
-        self.dots(2)
-        self.relay_out(2)
+        self.unit(3)
+        self.take(3, 1)
+        self.take(1, 1)
+        self.neighbours_out(2)
         self.owners_out(0)
-        self.last_ring()
-        self.neighbours_out(2)
-        self.dots(3)
-        self.relay_out(3)
+        self.unit(4)
+        self.take(2, 0)
+        self.take(3, 2)
+        self.take(1, 2)
+        self.neighbours_out(3)
         self.owners_out(1)
-        self.neighbours_out(3)
+        self.unit(5)
+        self.take(2, 3)
+        self.neighbours_out(4)
         self.owners_out(2)
+        self.unit(6)
+        self.take(2, 1)
+        self.take(2, 2)
+        self.neighbours_out(5)
         self.owners_out(3)
+        self.unit(7)
+        self.neighbours_out(6)
+        self.owners_out(4)
+        self.owners_out(5)
+        self.owners_out(6)
+        self.owners_out(7)
         self.owners_in()
+
+    def unit(self, w):
+        self.dots(w)
+        self.relay_out(w)
 
     def finish(self):
         for copy in self.sent:
@@ -408,39 +435,50 @@
             qkv[pl.ds(h * ROWS, ROWS), :] = head
 
 
-def attend(lengths, keys, values, qkv, mixed, out):
+def attend(lengths, keys, values, qkv, scored, weighed, mixed, out):
     share = HQ // KVH
     scale = 1.0 / math.sqrt(HD)
 
     @pl.loop(0, ROWS)
     def _(r):
-        valid = lax.broadcasted_iota(jnp.int32, (share, CACHE), 1) < lengths[r]
         for g in range(KVH):
-            columns = pl.ds(g * HD, HD)
-            span = pl.ds(g * share * ROWS + r, share, stride=ROWS)
-            query = qkv[span, :]
-            key_new = qkv[pl.ds((HQ + g) * ROWS + r, 1), :]
-            value_new = qkv[pl.ds((HQ + KVH + g) * ROWS + r, 1), :]
-            fresh = jnp.sum(query * key_new, axis=1, keepdims=True) * scale
-            scores = (
+            query = qkv[pl.ds(g * share * ROWS + r, share, stride=ROWS), :]
+            scored[r, pl.ds(g * share, share), :] = (
                 lax.dot_general(
                     query.astype(jnp.bfloat16),
-                    keys[r, :, columns],
+                    keys[r, :, pl.ds(g * HD, HD)],
                     (((1,), (1,)), ((), ())),
                     preferred_element_type=jnp.float32,
                 )
                 * scale
             )
-            scores = jnp.where(valid, scores, -jnp.inf)
-            top = jnp.maximum(jnp.max(scores, axis=1, keepdims=True), fresh)
-            probs = jnp.exp(scores - top)
-            pnew = jnp.exp(fresh - top)
-            total = jnp.sum(probs, axis=1, keepdims=True) + pnew
-            weights = (probs / total).astype(jnp.bfloat16)
-            wnew = (pnew / total).astype(jnp.bfloat16).astype(jnp.float32)
-            mixed[span, :] = (
-                jnp.dot(weights, values[r, :, columns], preferred_element_type=jnp.float32)
-                + wnew * value_new
+
+    @pl.loop(0, ROWS)
+    def _(r):
+        valid = lax.broadcasted_iota(jnp.int32, (HQ, CACHE), 1) < lengths[r]
+        query = qkv[pl.ds(r, HQ, stride=ROWS), :]
+        key_new = qkv[pl.ds(HQ * ROWS + r, KVH, stride=ROWS), :]
+        value_new = qkv[pl.ds((HQ + KVH) * ROWS + r, KVH, stride=ROWS), :]
+        both = query.reshape(KVH, share, HD) * key_new.reshape(KVH, 1, HD)
+        fresh = jnp.sum(both.reshape(HQ, HD), axis=1, keepdims=True) * scale
+        scores = jnp.where(valid, scored[r], -jnp.inf)
+        top = jnp.maximum(jnp.max(scores, axis=1, keepdims=True), fresh)
+        probs = jnp.exp(scores - top)
+        pnew = jnp.exp(fresh - top)
+        total = jnp.sum(probs, axis=1, keepdims=True) + pnew
+        weighed[r] = (probs / total).astype(jnp.bfloat16)
+        wnew = (pnew / total).astype(jnp.bfloat16).astype(jnp.float32)
+        added = wnew.reshape(KVH, share, 1) * value_new.reshape(KVH, 1, HD)
+        mixed[pl.ds(r, HQ, stride=ROWS), :] = added.reshape(HQ, HD)
+
+    @pl.loop(0, ROWS)
+    def _(r):
+        for g in range(KVH):
+            span = pl.ds(g * share * ROWS + r, share, stride=ROWS)
+            mixed[span, :] = mixed[span, :] + jnp.dot(
+                weighed[r, pl.ds(g * share, share), :],
+                values[r, :, pl.ds(g * HD, HD)],
+                preferred_element_type=jnp.float32,
             )
 
     for h in range(HQ):
@@ -465,6 +503,8 @@
     weight_out,
     turns,
     qkv,
+    scored,
+    weighed,
     mixed,
     loads,
     *refs,
@@ -495,7 +535,7 @@
     heads(first.owned, turns, qkv)
     fetch[1].wait()
     fetch[2].wait()
-    attend(lengths, keys, values, qkv, mixed, second.mine)
+    attend(lengths, keys, values, qkv, scored, weighed, mixed, second.mine)
     second.exchange()
     second.run(fetch[3].wait)
     out[...] = second.owned[...]
@@ -521,6 +561,8 @@
             pltpu.VMEM((DEPTH, 512), jnp.bfloat16),
             pltpu.VMEM((2, ROWS, HD), jnp.float32),
             pltpu.VMEM(((HQ + 2 * KVH) * ROWS, HD), jnp.float32),
+            pltpu.VMEM((ROWS, HQ, CACHE), jnp.float32),
+            pltpu.VMEM((ROWS, HQ, CACHE), jnp.bfloat16),
             pltpu.VMEM((HQ * ROWS, HD), jnp.float32),
             pltpu.SemaphoreType.DMA((4,)),
         ]

time: 151 us -> 123 us (0.81)
  Pallas kernels: 149 us -> 120 us
    pallas_call x1, Pallas kernels: 149 us -> 120 us  [on_device(): pl.pallas_call(layer, out_shape=jax.ShapeDtypeStruct((32, ROWS, 512), jnp...]
where the time goes in v4:
time: 123 us
  Pallas kernels  120 us (98%)
  local copies, waits for them, and re-layouts  1.67 us (1%)
    pallas_call x1, Pallas kernels, on_device(): pl.pallas_call(layer, out_shape=jax.ShapeDtypeStruct((32, ROWS, 512), jnp...  120 us

profile of v4, /device:TPU:1, one launch (start us, length us, event | category | flops | bytes accessed | tf_op | source)
XLA Modules:
  0.0 122.7 jit_solution(5895796994161624611)
XLA Ops:
  0.0 0.6 maximum_bitcast_fusion.freqs
  0.6 120.4 %layer.1 = bf16[32,8,512]{2,1,0:T(8,128)(2,1)} custom-call(s32[8]{0:T(128)} %lengths.1, bf16[8,16384]{1,0:T(8,128)(2,1)} %hidden.1, f32[1,16384]{1,0:T(1,128)} %bitcast.9, f32[1,128]{1,0:T(1,128)} %maximum_bitcast_fusion.freqs, bf16[576,4096]{1,0:T(8,128)(2,1)} %bitcast.7, bf16[8,512,1024]{2,1,0:T(8,128)(2,1)} %k_cache.1, bf16[8,512,1024]{2,1,0:T(8,128)(2,1)} %v_cache.1, ...), custom_call_target="tpu_custom_call" | custom-call | tf_op jit(solution)/shard_map/layer/pallas_call | solution.py:552
  121.0 1.7 %copy.9 = bf16[8,16384]{1,0:T(8,128)(2,1)} copy(bf16[8,16384]{1,0:T(8,128)(2,1)} %bitcast.8) | data formatting | bytes 524288
  (1 shorter events, 0.0 us)

commit v5 on v4

v5 whole, which is shorter than its diff:
```python
import math

import jax
import jax.numpy as jnp
import numpy as np
from jax import lax
from jax.experimental import pallas as pl
from jax.experimental.pallas import tpu as pltpu
from jax.sharding import PartitionSpec as P

HQ = 128
KVH = 8
HD = 128
ROWS = 8
CACHE = 512
DEPTH = 4096
QWIDE = 640

eps = 1e-05
theta = 500000.0

UNITS = (
    ((0, 0), (0, 3)),
    ((0, 1), (1, 0)),
    ((3, 0), (0, 2)),
    ((1, 3), (3, 3)),
    ((1, 1), (3, 1)),
    ((2, 0), (1, 2)),
    ((3, 2), (2, 3)),
    ((2, 1), (2, 2)),
)
DIRECT = (7,)
PLACE = {ur: (w, i) for w, unit in enumerate(UNITS) for i, ur in enumerate(unit)}


def remote(src, dst, send, recv, device):
    return pltpu.make_async_remote_copy(
        src_ref=src,
        dst_ref=dst,
        send_sem=send,
        recv_sem=recv,
        device_id=device,
        device_id_type=pl.DeviceIdType.MESH,
    )


class Here:
    def __init__(self):
        gx = lax.axis_index("gx")
        self.gx = gx
        self.z = lax.axis_index("gy")
        self.y = gx // 8
        self.x = (gx // 2) % 4
        self.c = gx % 2

    def device(self, dy=0, dx=0, dc=0, dz=0):
        y = (self.y + dy) % 4
        x = (self.x + dx) % 4
        c = (self.c + dc) % 2
        return ((y * 4 + x) * 2 + c, (self.z + dz) % 4)

    def greet(self):
        barrier = pltpu.get_barrier_semaphore()
        partners = [dict(dz=1), dict(dz=3), dict(dz=2), dict(dc=1)]
        partners += [dict(dx=1), dict(dx=3), dict(dy=1), dict(dy=3)]
        for partner in partners:
            pl.semaphore_signal(
                barrier,
                inc=1,
                device_id=self.device(**partner),
                device_id_type=pl.DeviceIdType.MESH,
            )

    def greeted(self):
        pl.semaphore_wait(pltpu.get_barrier_semaphore(), 8)


class Projection:
    def __init__(self, here, refs, rows, sems, weight, shared=None):
        self.here = here
        self.weight = weight
        self.shared = shared
        self.rows = rows
        self.mine, self.spread, self.partial, self.relay, self.last, self.ready, self.owned = refs
        self.tall = self.partial.shape[2]
        self.wide = self.owned.shape[2]
        self.got_z, self.got_near, self.got_far = (sems.at[k] for k in range(3))
        self.got_shard = lambda u, r: sems.at[3 + u * 4 + r]
        self.got_sibling = lambda w: sems.at[19 + w]
        self.got_relay = lambda w: sems.at[27 + w]
        self.got_last = lambda w: sems.at[35 + w]
        self.put_z, self.put_shard, self.put_sibling, self.put_sum, self.put_near, self.put_far = (
            sems.at[43 + k] for k in range(6)
        )

    SEMAPHORES = 49

    @staticmethod
    def scratch(wide, kind):
        tall = 128 if wide == 512 else 144
        return [
            pltpu.VMEM((4, 8, DEPTH), jnp.bfloat16),
            pltpu.VMEM((4, 8, DEPTH), jnp.bfloat16),
            pltpu.VMEM((8, 4, tall, HD), kind),
            pltpu.VMEM((8, tall, HD), kind),
            pltpu.VMEM((8, 2, tall, HD), kind),
            pltpu.VMEM((8, 4, 8, wide), jnp.bfloat16),
            pltpu.VMEM((32, 8, wide), jnp.bfloat16),
        ]

    def wait(self, ref, sem):
        remote(ref, ref, self.put_z, sem, self.here.device(dc=1)).wait_recv()

    def exchange(self):
        z = self.here.z
        for dz in (2, 1, 3):
            to = (z + dz) % 4
            remote(
                self.mine.at[to],
                self.spread.at[z],
                self.put_z,
                self.got_z,
                self.here.device(dz=dz),
            ).start()
        self.spread[z] = self.mine[z]

    def exchanged(self):
        self.wait(self.spread.at[pl.ds(0, 3)], self.got_z)
        for part in range(2):
            both = jnp.concatenate([self.spread[2 * part], self.spread[2 * part + 1]], axis=0)
            self.rows[pl.ds(self.start_of(0, 0, 0) + 16 * part, 16), :] = both

    @staticmethod
    def start_of(u, r, core):
        w, i = PLACE[(u, r)]
        return w * 128 + (i * 2 + core) * 32

    def slot(self, part, u, r, half=None):
        columns = pl.ds(0, DEPTH) if half is None else pl.ds(half * (DEPTH // 2), DEPTH // 2)
        return self.rows.at[pl.ds(self.start_of(u, r, 0) + part * 16, 16), columns]

    def hop(self, u, r, first, step, half=None):
        nu, nr = (u, (r - step) % 4) if first else ((u - step) % 4, r)
        for part in range(2):
            along = dict(dx=step) if first == (part == 0) else dict(dy=step)
            remote(
                self.slot(part, u, r, half),
                self.slot(part, nu, nr, half),
                self.put_shard,
                self.got_shard(nu, nr),
                self.here.device(**along),
            ).start()

    def to_sibling(self, u, r):
        remote(
            self.rows.at[pl.ds(self.start_of(u, r, 0), 32)],
            self.rows.at[pl.ds(self.start_of(u, r, 1), 32)],
            self.put_sibling,
            self.got_sibling(PLACE[(u, r)][0]),
            self.here.device(dc=1),
        ).start()

    def start(self):
        for first in (True, False):
            self.hop(0, 0, first, 1)
            self.hop(0, 0, first, -1)
        self.to_sibling(0, 0)

    def second(self, r):
        self.hop(0, r, False, 1)
        self.hop(0, r, False, -1)

    def take(self, u, r):
        self.wait(self.rows.at[pl.ds(self.start_of(u, r, 0), 32)], self.got_shard(u, r))
        if u in (1, 3):
            self.hop(u, r, False, 1 if u == 3 else -1, 0 if u == 3 else 1)
        elif u == 0 and r in (1, 3):
            self.hop(u, r, True, 1 if r == 3 else -1, 0 if r == 3 else 1)
        self.to_sibling(u, r)

    def dots(self, w):
        self.wait(self.rows.at[pl.ds(w * 128, 64)], self.got_sibling(w))

        @pl.loop(0, 2)
        def _(n):
            out = jnp.dot(
                self.rows[pl.ds(w * 128, 128), :],
                self.weight[:, pl.ds(pl.multiple_of(n * 256, 256), 256)],
                preferred_element_type=jnp.float32,
            ).reshape(4, 4, 8, 256)
            for d in range(4):
                for m in range(2):
                    block = out[:, d, :, m * HD : (m + 1) * HD].reshape(32, HD)
                    at = pl.ds(pl.multiple_of(n * 64 + m * 32, 32), 32)
                    self.partial[w, d, at, :] = block.astype(self.partial.dtype)

        if self.shared is not None:
            own = jnp.concatenate(
                [self.rows[pl.ds(w * 128 + i * 64, 32), :] for i in range(2)], axis=0
            )
            out = lax.dot_general(
                own, self.shared[...], (((1,), (1,)), ((), ())), preferred_element_type=jnp.float32
            ).reshape(2, 4, 8, HD)
            for d in range(4):
                self.partial[w, d, pl.ds(128, 16), :] = out[:, d].reshape(16, HD)

    def sum_copy(self, src, dst, sem, dz):
        remote(src, dst, self.put_sum, sem, self.here.device(dz=dz)).start()

    def relay_out(self, w):
        z = self.here.z
        far = (z + 2) % 4
        half = self.tall // 2
        if w in DIRECT:
            self.sum_copy(self.partial.at[w, far], self.relay.at[w], self.got_relay(w), 2)
            for side, dz in ((0, 1), (1, -1)):
                to = (z + dz) % 4
                self.sum_copy(
                    self.partial.at[w, to], self.last.at[w, side], self.got_last(w), dz
                )
            return
        for side, dz in ((0, 1), (1, -1)):
            at = pl.ds(half * side, half)
            self.sum_copy(
                self.partial.at[w, far, at], self.relay.at[w, at], self.got_relay(w), dz
            )

    def neighbours_out(self, w):
        if w in DIRECT:
            return
        self.wait(self.relay.at[w], self.got_relay(w))
        half = self.tall // 2
        for side, dz in ((0, 1), (1, -1)):
            to = (self.here.z + dz) % 4
            at = pl.ds(half * side, half)
            total = self.partial[w, to, at, :].astype(jnp.float32) + self.relay[w, at, :].astype(
                jnp.float32
            )
            self.partial[w, to, at, :] = total.astype(self.partial.dtype)
            self.sum_copy(self.partial.at[w, to], self.last.at[w, side], self.got_last(w), dz)

    def owners_out(self, w):
        here = self.here
        self.wait(self.last.at[w], self.got_last(w))
        total = self.partial[w, here.z].astype(jnp.float32)
        for side in range(2):
            total = total + self.last[w, side].astype(jnp.float32)
        if w in DIRECT:
            self.wait(self.relay.at[w], self.got_relay(w))
            total = total + self.relay[w].astype(jnp.float32)
        total = total.astype(jnp.bfloat16).astype(jnp.float32)
        for n in range(4):
            block = total[n * 32 : (n + 1) * 32].reshape(4, 8, HD)
            self.ready[w, :, :, pl.ds(n * HD, HD)] = block.astype(jnp.bfloat16)
        if self.shared is not None:
            for i in range(2):
                block = total[128 + i * 8 : 136 + i * 8]
                self.ready[w, 2 * i, :, pl.ds(512, HD)] = block.astype(jnp.bfloat16)
        for i, (u, r) in enumerate(UNITS[w]):
            for core in range(2):
                j = i * 2 + core
                if w == 0 and j == 0:
                    self.owned[here.gx] = self.ready[0, 0]
                    continue
                wide = pl.ds(0, 512 if core else self.wide)
                remote(
                    self.ready.at[w, j, :, wide],
                    self.owned.at[here.gx, :, wide],
                    self.put_far if core else self.put_near,
                    self.got_far if core else self.got_near,
                    self.owner(u, r, core),
                ).start()

    def owner(self, u, r, core):
        first = self.here.z < 2
        dy = jnp.where(first, u, r)
        dx = jnp.where(first, r, u)
        return self.here.device(dy, dx, core)

    def near(self):
        return self.owned.at[pl.ds(0, 15)]

    def far(self):
        return self.owned.at[pl.ds(0, 16), :, pl.ds(0, 512)]

    def owners_in(self):
        self.wait(self.near(), self.got_near)
        self.wait(self.far(), self.got_far)

    def unit(self, w):
        self.dots(w)
        self.relay_out(w)

    def run(self, weight_in):
        self.exchanged()
        self.start()
        self.take(0, 3)
        self.take(0, 1)
        self.second(3)
        self.second(1)
        weight_in()
        self.unit(0)
        self.take(3, 0)
        self.take(1, 0)
        self.unit(1)
        self.take(0, 2)
        self.second(2)
        self.neighbours_out(0)
        self.unit(2)
        self.take(3, 3)
        self.take(1, 3)
        self.neighbours_out(1)
        self.unit(3)
        self.neighbours_out(2)
        self.take(3, 1)
        self.take(1, 1)
        self.owners_out(0)
        self.unit(4)
        self.neighbours_out(3)
        self.take(2, 0)
        self.take(3, 2)
        self.take(1, 2)
        self.owners_out(1)
        self.unit(5)
        self.take(2, 3)
        self.neighbours_out(4)
        self.owners_out(2)
        self.unit(6)
        self.neighbours_out(5)
        self.take(2, 1)
        self.take(2, 2)
        self.unit(7)
        self.owners_out(3)
        self.neighbours_out(6)
        self.owners_out(4)
        self.owners_out(5)
        self.owners_out(6)
        self.owners_out(7)
        self.owners_in()

    def finish(self):
        for ref, sem in (
            (self.mine.at[pl.ds(0, 3)], self.put_z),
            (self.rows.at[pl.ds(0, 480)], self.put_shard),
            (self.rows.at[pl.ds(0, 512)], self.put_sibling),
            (self.partial.at[pl.ds(0, 6)], self.put_sum),
            (self.near(), self.put_near),
            (self.far(), self.put_far),
        ):
            remote(ref, ref, sem, self.got_z, self.here.device(dc=1)).wait_send()


def normalized(step, hidden, gain):
    widened = hidden[...].astype(jnp.float32)
    scale = lax.rsqrt(jnp.mean(widened * widened, axis=-1, keepdims=True) + eps)
    for z in range(4):
        columns = pl.ds(z * DEPTH, DEPTH)
        step.mine[z] = (hidden[:, columns].astype(jnp.float32) * scale * gain[:, columns]).astype(
            jnp.bfloat16
        )


def turn(lengths, freqs, turns):
    row = lax.broadcasted_iota(jnp.int32, (ROWS, HD), 0)
    lane = lax.broadcasted_iota(jnp.int32, (ROWS, HD), 1)
    position = jnp.zeros((ROWS, HD), jnp.float32)
    for r in range(ROWS):
        position = jnp.where(row == r, lengths[r].astype(jnp.float32), position)
    angle = position * freqs[...]
    turns[0] = jnp.cos(angle)
    turns[1] = jnp.where(lane < HD // 2, -jnp.sin(angle), jnp.sin(angle))


def heads(core, owned, turns, qkv):
    for pair in range(16):
        even = owned[2 * pair, :, pl.ds(0, 512)].astype(jnp.float32)
        odd = owned[2 * pair + 1, :, pl.ds(0, 512)].astype(jnp.float32)
        between = owned[2 * pair + core, :, pl.ds(512, HD)].astype(jnp.float32)
        for t in range(9):
            if t < 4:
                head = even[:, t * HD : (t + 1) * HD]
            elif t > 4:
                head = odd[:, (t - 5) * HD : (t - 4) * HD]
            else:
                head = between
            h = pair * 9 + t
            if h < HQ + KVH:
                head = head * turns[0] + pltpu.roll(head, HD // 2, 1) * turns[1]
                head = head.astype(jnp.bfloat16).astype(jnp.float32)
            qkv[pl.ds(h * ROWS, ROWS), :] = head


def attend(lengths, keys, values, qkv, scored, weighed, mixed, out):
    share = HQ // KVH
    scale = 1.0 / math.sqrt(HD)

    @pl.loop(0, ROWS)
    def _(r):
        for g in range(KVH):
            query = qkv[pl.ds(g * share * ROWS + r, share, stride=ROWS), :]
            scored[r, pl.ds(g * share, share), :] = (
                lax.dot_general(
                    query.astype(jnp.bfloat16),
                    keys[r, :, pl.ds(g * HD, HD)],
                    (((1,), (1,)), ((), ())),
                    preferred_element_type=jnp.float32,
                )
                * scale
            )

    @pl.loop(0, ROWS)
    def _(r):
        valid = lax.broadcasted_iota(jnp.int32, (HQ, CACHE), 1) < lengths[r]
        query = qkv[pl.ds(r, HQ, stride=ROWS), :]
        key_new = qkv[pl.ds(HQ * ROWS + r, KVH, stride=ROWS), :]
        value_new = qkv[pl.ds((HQ + KVH) * ROWS + r, KVH, stride=ROWS), :]
        both = query.reshape(KVH, share, HD) * key_new.reshape(KVH, 1, HD)
        fresh = jnp.sum(both.reshape(HQ, HD), axis=1, keepdims=True) * scale
        scores = jnp.where(valid, scored[r], -jnp.inf)
        top = jnp.maximum(jnp.max(scores, axis=1, keepdims=True), fresh)
        probs = jnp.exp(scores - top)
        pnew = jnp.exp(fresh - top)
        total = jnp.sum(probs, axis=1, keepdims=True) + pnew
        weighed[r] = (probs / total).astype(jnp.bfloat16)
        wnew = (pnew / total).astype(jnp.bfloat16).astype(jnp.float32)
        added = wnew.reshape(KVH, share, 1) * value_new.reshape(KVH, 1, HD)
        mixed[pl.ds(r, HQ, stride=ROWS), :] = added.reshape(HQ, HD)

    @pl.loop(0, ROWS)
    def _(r):
        for g in range(KVH):
            span = pl.ds(g * share * ROWS + r, share, stride=ROWS)
            mixed[span, :] = mixed[span, :] + jnp.dot(
                weighed[r, pl.ds(g * share, share), :],
                values[r, :, pl.ds(g * HD, HD)],
                preferred_element_type=jnp.float32,
            )

    for h in range(HQ):
        out[h // 32, :, pl.ds(h % 32 * HD, HD)] = mixed[pl.ds(h * ROWS, ROWS), :].astype(
            jnp.bfloat16
        )


def transposed(raw, weight):
    @pl.loop(0, DEPTH // 512)
    def _(k):
        for n in range(4):
            at = pl.ds(pl.multiple_of(k * 512, 512), 512)
            weight[at, pl.ds(n * HD, HD)] = raw[pl.ds(n * HD, HD), at].T


def layer(
    lengths,
    hidden,
    gain,
    freqs,
    w_qkv,
    k_cache,
    v_cache,
    w_out,
    out,
    later_rows,
    shared,
    weight_in,
    keys,
    values,
    weight_out,
    turns,
    qkv,
    scored,
    weighed,
    mixed,
    rows,
    loads,
    sems,
    *refs,
):
    here = Here()
    here.greet()
    count = len(refs) // 2
    first = Projection(here, refs[:count], rows, sems, weight_in, shared)
    second = Projection(here, refs[count:], later_rows, sems, weight_out)
    raw = later_rows.at[pl.ds(0, 512)]
    c = here.c
    half = w_qkv.at[pl.ds(pl.multiple_of((1 - c) * 512, 64), 64)]
    place = shared.at[pl.ds(pl.multiple_of(c * 64, 64), 64)]
    fetch = [
        pltpu.make_async_copy(
            w_qkv.at[pl.ds(pl.multiple_of(c * 64, 64), 512)], raw, loads.at[0]
        ),
        pltpu.make_async_copy(half, place, loads.at[1]),
        pltpu.make_async_copy(k_cache, keys, loads.at[2]),
        pltpu.make_async_copy(v_cache, values, loads.at[3]),
        pltpu.make_async_copy(w_out, weight_out, loads.at[4]),
    ]
    for copy in fetch:
        copy.start()
    normalized(first, hidden, gain)
    here.greeted()
    first.exchange()
    swap = remote(half, place, loads.at[5], loads.at[6], here.device(dc=1))
    swap.start()
    turn(lengths, freqs, turns)
    fetch[0].wait()
    transposed(raw, weight_in)
    fetch[1].wait()
    first.run(swap.wait)
    heads(c, first.owned, turns, qkv)
    fetch[2].wait()
    fetch[3].wait()
    attend(lengths, keys, values, qkv, scored, weighed, mixed, second.mine)
    first.finish()
    second.exchange()
    second.run(fetch[4].wait)
    out[...] = second.owned[...]
    second.finish()


def on_device(hidden_in, norm_gain, w_qkv, k_cache, v_cache, lengths, w_out):
    freqs = theta ** (-2.0 * (np.arange(HD) % (HD // 2)) / HD)
    freqs = jnp.asarray(freqs.astype(np.float32).reshape(1, HD))
    vmem = pl.BlockSpec(memory_space=pltpu.VMEM)
    hbm = pl.BlockSpec(memory_space=pl.ANY)
    blocks = pl.pallas_call(
        layer,
        out_shape=jax.ShapeDtypeStruct((32, ROWS, 512), jnp.bfloat16),
        in_specs=[pl.BlockSpec(memory_space=pltpu.SMEM), vmem, vmem, vmem, hbm, hbm, hbm, hbm],
        out_specs=vmem,
        scratch_shapes=[
            pltpu.VMEM((1024, DEPTH), jnp.bfloat16),
            pltpu.VMEM((HD, DEPTH), jnp.bfloat16),
            pltpu.VMEM((DEPTH, 512), jnp.bfloat16),
            pltpu.VMEM((ROWS, CACHE, KVH * HD), jnp.bfloat16),
            pltpu.VMEM((ROWS, CACHE, KVH * HD), jnp.bfloat16),
            pltpu.VMEM((DEPTH, 512), jnp.bfloat16),
            pltpu.VMEM((2, ROWS, HD), jnp.float32),
            pltpu.VMEM(((HQ + 2 * KVH) * ROWS, HD), jnp.float32),
            pltpu.VMEM((ROWS, HQ, CACHE), jnp.float32),
            pltpu.VMEM((ROWS, HQ, CACHE), jnp.bfloat16),
            pltpu.VMEM((HQ * ROWS, HD), jnp.float32),
            pltpu.VMEM((1024, DEPTH), jnp.bfloat16),
            pltpu.SemaphoreType.DMA((7,)),
            pltpu.SemaphoreType.DMA((Projection.SEMAPHORES,)),
        ]
        + Projection.scratch(QWIDE, jnp.float32)
        + Projection.scratch(512, jnp.bfloat16),
        compiler_params=pltpu.CompilerParams(
            collective_id=0, has_side_effects=True, vmem_limit_bytes=60 * 1024 * 1024
        ),
        name="layer",
    )(lengths, hidden_in, norm_gain.reshape(1, -1), freqs, w_qkv.T, k_cache, v_cache, w_out)
    return blocks.transpose(1, 0, 2).reshape(ROWS, 32 * 512)


def solution(mesh):
    return jax.shard_map(
        on_device,
        mesh=mesh,
        in_specs=(
            P(("gx", "gy"), None),
            P(),
            P("gy", "gx"),
            P(("gx", "gy"), None, None),
            P(("gx", "gy"), None, None),
            P(("gx", "gy")),
            P("gy", "gx"),
        ),
        out_specs=P(("gx", "gy"), None),
        check_vma=False,
    )
```

time: 123 us -> 111 us (0.902)
  Pallas kernels: 120 us -> 109 us
    pallas_call x1, Pallas kernels: 120 us -> 109 us  [on_device(): pl.pallas_call(layer, out_shape=jax.ShapeDtypeStruct((32, ROWS, 512), jnp...]
where the time goes in v5:
time: 111 us
  Pallas kernels  109 us (98%)
  local copies, waits for them, and re-layouts  1.67 us (2%)
    pallas_call x1, Pallas kernels, on_device(): pl.pallas_call(layer, out_shape=jax.ShapeDtypeStruct((32, ROWS, 512), jnp...  109 us

profile of v5, /device:TPU:1, one launch (start us, length us, event | category | flops | bytes accessed | tf_op | source)
XLA Modules:
  0.0 110.8 jit_solution(4635339145296559468)
XLA Ops:
  0.0 109.1 %layer.1 = bf16[32,8,512]{2,1,0:T(8,128)(2,1)} custom-call(s32[8]{0:T(128)} %lengths.1, bf16[8,16384]{1,0:T(8,128)(2,1)} %hidden.1, f32[1,16384]{1,0:T(1,128)} %bitcast.7, f32[1,128]{1,0:T(1,128)} %constant.2.clone.freqs, bf16[576,4096]{1,0:T(8,128)(2,1)} %bitcast.5, bf16[8,512,1024]{2,1,0:T(8,128)(2,1)} %k_cache.1, bf16[8,512,1024]{2,1,0:T(8,128)(2,1)} %v_cache.1, ...), custom_call_target="tpu_custom_call" | custom-call | tf_op jit(solution)/shard_map/layer/pallas_call | solution.py:525
  109.1 1.7 %copy.10 = bf16[8,16384]{1,0:T(8,128)(2,1)} copy(bf16[8,16384]{1,0:T(8,128)(2,1)} %bitcast.6) | data formatting | bytes 524288

commit v6 on v5

--- a/solution.py
+++ b/solution.py
@@ -29,7 +29,8 @@
     ((3, 2), (2, 3)),
     ((2, 1), (2, 2)),
 )
-DIRECT = (7,)
+COUNT = len(UNITS)
+BASE = [64 * sum(len(unit) for unit in UNITS[:w]) for w in range(COUNT)]
 PLACE = {ur: (w, i) for w, unit in enumerate(UNITS) for i, ur in enumerate(unit)}
 
 
@@ -81,19 +82,19 @@
         self.weight = weight
         self.shared = shared
         self.rows = rows
-        self.mine, self.spread, self.partial, self.relay, self.last, self.ready, self.owned = refs
-        self.tall = self.partial.shape[2]
+        self.mine, self.spread, self.partial, self.far_sum, self.last, self.ready, self.owned = refs
         self.wide = self.owned.shape[2]
+        self.tall = [len(unit) * (64 if shared is None else 72) for unit in UNITS]
         self.got_z, self.got_near, self.got_far = (sems.at[k] for k in range(3))
         self.got_shard = lambda u, r: sems.at[3 + u * 4 + r]
         self.got_sibling = lambda w: sems.at[19 + w]
-        self.got_relay = lambda w: sems.at[27 + w]
-        self.got_last = lambda w: sems.at[35 + w]
+        self.got_sum = lambda w: sems.at[19 + COUNT + w]
+        self.got_last = lambda w: sems.at[19 + 2 * COUNT + w]
         self.put_z, self.put_shard, self.put_sibling, self.put_sum, self.put_near, self.put_far = (
-            sems.at[43 + k] for k in range(6)
+            sems.at[19 + 3 * COUNT + k] for k in range(6)
         )
 
-    SEMAPHORES = 49
+    SEMAPHORES = 25 + 3 * COUNT
 
     @staticmethod
     def scratch(wide, kind):
@@ -101,31 +102,29 @@
         return [
             pltpu.VMEM((4, 8, DEPTH), jnp.bfloat16),
             pltpu.VMEM((4, 8, DEPTH), jnp.bfloat16),
-            pltpu.VMEM((8, 4, tall, HD), kind),
-            pltpu.VMEM((8, tall, HD), kind),
-            pltpu.VMEM((8, 2, tall, HD), kind),
-            pltpu.VMEM((8, 4, 8, wide), jnp.bfloat16),
+            pltpu.VMEM((COUNT, 4, tall, HD), kind),
+            pltpu.VMEM((COUNT, tall, HD), kind),
+            pltpu.VMEM((COUNT, 2, tall, HD), kind),
+            pltpu.VMEM((COUNT, 4, 8, wide), jnp.bfloat16),
             pltpu.VMEM((32, 8, wide), jnp.bfloat16),
         ]
 
     def wait(self, ref, sem):
         remote(ref, ref, self.put_z, sem, self.here.device(dc=1)).wait_recv()
 
-    def exchange(self):
+    def exchange(self, dz):
         z = self.here.z
-        for dz in (2, 1, 3):
-            to = (z + dz) % 4
-            remote(
-                self.mine.at[to],
-                self.spread.at[z],
-                self.put_z,
-                self.got_z,
-                self.here.device(dz=dz),
-            ).start()
-        self.spread[z] = self.mine[z]
+        remote(
+            self.mine.at[(z + dz) % 4],
+            self.spread.at[z],
+            self.put_z,
+            self.got_z,
+            self.here.device(dz=dz),
+        ).start()
 
     def exchanged(self):
-        self.wait(self.spread.at[pl.ds(0, 3)], self.got_z)
+        three = self.spread.at[pl.ds(0, 3)]
+        self.wait(three, self.got_z)
         for part in range(2):
             both = jnp.concatenate([self.spread[2 * part], self.spread[2 * part + 1]], axis=0)
             self.rows[pl.ds(self.start_of(0, 0, 0) + 16 * part, 16), :] = both
@@ -133,7 +132,7 @@
     @staticmethod
     def start_of(u, r, core):
         w, i = PLACE[(u, r)]
-        return w * 128 + (i * 2 + core) * 32
+        return BASE[w] + (i * 2 + core) * 32
 
     def slot(self, part, u, r, half=None):
         columns = pl.ds(0, DEPTH) if half is None else pl.ds(half * (DEPTH // 2), DEPTH // 2)
@@ -179,82 +178,70 @@
         self.to_sibling(u, r)
 
     def dots(self, w):
-        self.wait(self.rows.at[pl.ds(w * 128, 64)], self.got_sibling(w))
+        pairs = len(UNITS[w])
+        high = 16 * pairs
+        self.wait(self.rows.at[pl.ds(BASE[w], 32 * pairs)], self.got_sibling(w))
 
         @pl.loop(0, 2)
         def _(n):
             out = jnp.dot(
-                self.rows[pl.ds(w * 128, 128), :],
+                self.rows[pl.ds(BASE[w], 64 * pairs), :],
                 self.weight[:, pl.ds(pl.multiple_of(n * 256, 256), 256)],
                 preferred_element_type=jnp.float32,
-            ).reshape(4, 4, 8, 256)
+            ).reshape(2 * pairs, 4, 8, 256)
             for d in range(4):
                 for m in range(2):
-                    block = out[:, d, :, m * HD : (m + 1) * HD].reshape(32, HD)
-                    at = pl.ds(pl.multiple_of(n * 64 + m * 32, 32), 32)
+                    block = out[:, d, :, m * HD : (m + 1) * HD].reshape(high, HD)
+                    at = pl.ds(pl.multiple_of((n * 2 + m) * high, high), high)
                     self.partial[w, d, at, :] = block.astype(self.partial.dtype)
 
         if self.shared is not None:
-            own = jnp.concatenate(
-                [self.rows[pl.ds(w * 128 + i * 64, 32), :] for i in range(2)], axis=0
-            )
+            own = [self.rows[pl.ds(BASE[w] + i * 64, 32), :] for i in range(pairs)]
             out = lax.dot_general(
-                own, self.shared[...], (((1,), (1,)), ((), ())), preferred_element_type=jnp.float32
-            ).reshape(2, 4, 8, HD)
+                jnp.concatenate(own, axis=0) if pairs > 1 else own[0],
+                self.shared[...],
+                (((1,), (1,)), ((), ())),
+                preferred_element_type=jnp.float32,
+            ).reshape(pairs, 4, 8, HD)
             for d in range(4):
-                self.partial[w, d, pl.ds(128, 16), :] = out[:, d].reshape(16, HD)
+                at = pl.ds(4 * high, 8 * pairs)
+                self.partial[w, d, at, :] = out[:, d].reshape(8 * pairs, HD)
 
     def sum_copy(self, src, dst, sem, dz):
         remote(src, dst, self.put_sum, sem, self.here.device(dz=dz)).start()
 
-    def relay_out(self, w):
+    def sum_out(self, w):
         z = self.here.z
-        far = (z + 2) % 4
-        half = self.tall // 2
-        if w in DIRECT:
-            self.sum_copy(self.partial.at[w, far], self.relay.at[w], self.got_relay(w), 2)
-            for side, dz in ((0, 1), (1, -1)):
-                to = (z + dz) % 4
-                self.sum_copy(
-                    self.partial.at[w, to], self.last.at[w, side], self.got_last(w), dz
-                )
-            return
+        at = pl.ds(0, self.tall[w])
+        self.sum_copy(
+            self.partial.at[w, (z + 2) % 4, at], self.far_sum.at[w, at], self.got_sum(w), 2
+        )
         for side, dz in ((0, 1), (1, -1)):
-            at = pl.ds(half * side, half)
             self.sum_copy(
-                self.partial.at[w, far, at], self.relay.at[w, at], self.got_relay(w), dz
+                self.partial.at[w, (z + dz) % 4, at],
+                self.last.at[w, side, at],
+                self.got_last(w),
+                dz,
             )
-
-    def neighbours_out(self, w):
-        if w in DIRECT:
-            return
-        self.wait(self.relay.at[w], self.got_relay(w))
-        half = self.tall // 2
-        for side, dz in ((0, 1), (1, -1)):
-            to = (self.here.z + dz) % 4
-            at = pl.ds(half * side, half)
-            total = self.partial[w, to, at, :].astype(jnp.float32) + self.relay[w, at, :].astype(
-                jnp.float32
-            )
-            self.partial[w, to, at, :] = total.astype(self.partial.dtype)
-            self.sum_copy(self.partial.at[w, to], self.last.at[w, side], self.got_last(w), dz)
 
     def owners_out(self, w):
         here = self.here
-        self.wait(self.last.at[w], self.got_last(w))
-        total = self.partial[w, here.z].astype(jnp.float32)
+        pairs = len(UNITS[w])
+        at = pl.ds(0, self.tall[w])
+        self.wait(self.last.at[w, :, at], self.got_last(w))
+        total = self.partial[w, here.z, at].astype(jnp.float32)
         for side in range(2):
-            total = total + self.last[w, side].astype(jnp.float32)
-        if w in DIRECT:
-            self.wait(self.relay.at[w], self.got_relay(w))
-            total = total + self.relay[w].astype(jnp.float32)
+            total = total + self.last[w, side, at].astype(jnp.float32)
+        self.wait(self.far_sum.at[w, at], self.got_sum(w))
+        total = total + self.far_sum[w, at].astype(jnp.float32)
         total = total.astype(jnp.bfloat16).astype(jnp.float32)
+        high = 16 * pairs
         for n in range(4):
-            block = total[n * 32 : (n + 1) * 32].reshape(4, 8, HD)
-            self.ready[w, :, :, pl.ds(n * HD, HD)] = block.astype(jnp.bfloat16)
+            block = total[n * high : (n + 1) * high].reshape(2 * pairs, 8, HD)
+            self.ready[w, pl.ds(0, 2 * pairs), :, pl.ds(n * HD, HD)] = block.astype(jnp.bfloat16)
         if self.shared is not None:
-            for i in range(2):
-                block = total[128 + i * 8 : 136 + i * 8]
+            for i in range(pairs):
+                block = total[4 * high + i * 8 : 4 * high + i * 8 + 8]
                 self.ready[w, 2 * i, :, pl.ds(512, HD)] = block.astype(jnp.bfloat16)
         for i, (u, r) in enumerate(UNITS[w]):
             for core in range(2):
@@ -289,7 +276,7 @@
 
     def unit(self, w):
         self.dots(w)
-        self.relay_out(w)
+        self.sum_out(w)
 
     def run(self, weight_in):
         self.exchanged()
@@ -305,49 +292,47 @@
         self.unit(1)
         self.take(0, 2)
         self.second(2)
-        self.neighbours_out(0)
         self.unit(2)
         self.take(3, 3)
         self.take(1, 3)
-        self.neighbours_out(1)
         self.unit(3)
-        self.neighbours_out(2)
         self.take(3, 1)
         self.take(1, 1)
         self.owners_out(0)
         self.unit(4)
-        self.neighbours_out(3)
         self.take(2, 0)
         self.take(3, 2)
         self.take(1, 2)
         self.owners_out(1)
         self.unit(5)
         self.take(2, 3)
-        self.neighbours_out(4)
-        self.owners_out(2)
         self.unit(6)
-        self.neighbours_out(5)
         self.take(2, 1)
         self.take(2, 2)
+        self.owners_out(2)
         self.unit(7)
         self.owners_out(3)
-        self.neighbours_out(6)
         self.owners_out(4)
         self.owners_out(5)
         self.owners_out(6)
         self.owners_out(7)
         self.owners_in()
 
+    def wait_sent(self, ref, sem):
+        remote(ref, ref, sem, self.got_z, self.here.device(dc=1)).wait_send()
+
+    def finish_exchange(self):
+        self.wait_sent(self.mine.at[pl.ds(0, 3)], self.put_z)
+
     def finish(self):
         for ref, sem in (
-            (self.mine.at[pl.ds(0, 3)], self.put_z),
             (self.rows.at[pl.ds(0, 480)], self.put_shard),
             (self.rows.at[pl.ds(0, 512)], self.put_sibling),
             (self.partial.at[pl.ds(0, 6)], self.put_sum),
             (self.near(), self.put_near),
             (self.far(), self.put_far),
         ):
-            remote(ref, ref, sem, self.got_z, self.here.device(dc=1)).wait_send()
+            self.wait_sent(ref, sem)
 
 
 def normalized(step, hidden, gain):
@@ -390,56 +375,64 @@
             qkv[pl.ds(h * ROWS, ROWS), :] = head
 
 
-def attend(lengths, keys, values, qkv, scored, weighed, mixed, out):
+def attend(z, lengths, keys, values, qkv, scored, weighed, mixed, out):
     share = HQ // KVH
     scale = 1.0 / math.sqrt(HD)
-
-    @pl.loop(0, ROWS)
-    def _(r):
-        for g in range(KVH):
-            query = qkv[pl.ds(g * share * ROWS + r, share, stride=ROWS), :]
-            scored[r, pl.ds(g * share, share), :] = (
-                lax.dot_general(
-                    query.astype(jnp.bfloat16),
-                    keys[r, :, pl.ds(g * HD, HD)],
-                    (((1,), (1,)), ((), ())),
+    batch = 8
+
+    def columns(g):
+        return pl.ds(pl.multiple_of((2 * z + g) * HD, HD), HD)
+
+    def span(g, r):
+        return pl.ds((2 * z + g) * share * ROWS + r, share, stride=ROWS)
+
+    @pl.loop(0, ROWS // batch)
+    def _(k):
+        for b in range(batch):
+            r = k * batch + b
+            for g in range(2):
+                scored[r, pl.ds(g * share, share), :] = (
+                    lax.dot_general(
+                        qkv[span(g, r), :].astype(jnp.bfloat16),
+                        keys[r, :, columns(g)],
+                        (((1,), (1,)), ((), ())),
+                        preferred_element_type=jnp.float32,
+                    )
+                    * scale
+                )
+
+    @pl.loop(0, ROWS // batch)
+    def _(k):
+        for b in range(batch):
+            r = k * batch + b
+            valid = lax.broadcasted_iota(jnp.int32, (share, CACHE), 1) < lengths[r]
+            for g in range(2):
+                key_new = qkv[pl.ds((HQ + 2 * z + g) * ROWS + r, 1), :]
+                value_new = qkv[pl.ds((HQ + KVH + 2 * z + g) * ROWS + r, 1), :]
+                fresh = jnp.sum(qkv[span(g, r), :] * key_new, axis=1, keepdims=True) * scale
+                scores = jnp.where(valid, scored[r, pl.ds(g * share, share), :], -jnp.inf)
+                top = jnp.maximum(jnp.max(scores, axis=1, keepdims=True), fresh)
+                probs = jnp.exp(scores - top)
+                pnew = jnp.exp(fresh - top)
+                total = jnp.sum(probs, axis=1, keepdims=True) + pnew
+                weighed[r, pl.ds(g * share, share), :] = (probs / total).astype(jnp.bfloat16)
+                wnew = (pnew / total).astype(jnp.bfloat16).astype(jnp.float32)
+                mixed[pl.ds(g * share * ROWS + r, share, stride=ROWS), :] = wnew * value_new
+
+    @pl.loop(0, ROWS // batch)
+    def _(k):
+        for b in range(batch):
+            r = k * batch + b
+            for g in range(2):
+                at = pl.ds(g * share * ROWS + r, share, stride=ROWS)
+                mixed[at, :] = mixed[at, :] + jnp.dot(
+                    weighed[r, pl.ds(g * share, share), :],
+                    values[r, :, columns(g)],
                     preferred_element_type=jnp.float32,
                 )
-                * scale
-            )
-
-    @pl.loop(0, ROWS)
-    def _(r):
-        valid = lax.broadcasted_iota(jnp.int32, (HQ, CACHE), 1) < lengths[r]
-        query = qkv[pl.ds(r, HQ, stride=ROWS), :]
-        key_new = qkv[pl.ds(HQ * ROWS + r, KVH, stride=ROWS), :]
-        value_new = qkv[pl.ds((HQ + KVH) * ROWS + r, KVH, stride=ROWS), :]
-        both = query.reshape(KVH, share, HD) * key_new.reshape(KVH, 1, HD)
-        fresh = jnp.sum(both.reshape(HQ, HD), axis=1, keepdims=True) * scale
-        scores = jnp.where(valid, scored[r], -jnp.inf)
-        top = jnp.maximum(jnp.max(scores, axis=1, keepdims=True), fresh)
-        probs = jnp.exp(scores - top)
-        pnew = jnp.exp(fresh - top)
-        total = jnp.sum(probs, axis=1, keepdims=True) + pnew
-        weighed[r] = (probs / total).astype(jnp.bfloat16)
-        wnew = (pnew / total).astype(jnp.bfloat16).astype(jnp.float32)
-        added = wnew.reshape(KVH, share, 1) * value_new.reshape(KVH, 1, HD)
-        mixed[pl.ds(r, HQ, stride=ROWS), :] = added.reshape(HQ, HD)
-
-    @pl.loop(0, ROWS)
-    def _(r):
-        for g in range(KVH):
-            span = pl.ds(g * share * ROWS + r, share, stride=ROWS)
-            mixed[span, :] = mixed[span, :] + jnp.dot(
-                weighed[r, pl.ds(g * share, share), :],
-                values[r, :, pl.ds(g * HD, HD)],
-                preferred_element_type=jnp.float32,
-            )
-
-    for h in range(HQ):
-        out[h // 32, :, pl.ds(h % 32 * HD, HD)] = mixed[pl.ds(h * ROWS, ROWS), :].astype(
-            jnp.bfloat16
-        )
+
+    for h in range(2 * share):
+        out[z, :, pl.ds(h * HD, HD)] = mixed[pl.ds(h * ROWS, ROWS), :].astype(jnp.bfloat16)
 
 
 def transposed(raw, weight):
@@ -451,15 +444,20 @@
 
 
 def layer(
-    lengths,
-    hidden,
-    gain,
-    freqs,
+    lengths_in,
+    hidden_in,
+    gain_in,
+    freqs_in,
     w_qkv,
     k_cache,
     v_cache,
     w_out,
     out,
+    lengths,
+    hidden,
+    gain,
+    freqs,
+    small,
     later_rows,
     shared,
     weight_in,
@@ -478,6 +476,14 @@
 ):
     here = Here()
     here.greet()
+    staged = [
+        pltpu.make_async_copy(hidden_in, hidden, small.at[0]),
+        pltpu.make_async_copy(gain_in, gain, small.at[1]),
+        pltpu.make_async_copy(freqs_in, freqs, small.at[2]),
+        pltpu.make_async_copy(lengths_in, lengths, small.at[3]),
+    ]
+    for copy in staged:
+        copy.start()
     count = len(refs) // 2
     first = Projection(here, refs[:count], rows, sems, weight_in, shared)
     second = Projection(here, refs[count:], later_rows, sems, weight_out)
@@ -494,13 +500,19 @@
         pltpu.make_async_copy(v_cache, values, loads.at[3]),
         pltpu.make_async_copy(w_out, weight_out, loads.at[4]),
     ]
-    for copy in fetch:
+    for copy in staged:
+        copy.wait()
+    for copy in fetch[:2]:
         copy.start()
     normalized(first, hidden, gain)
     here.greeted()
-    first.exchange()
+    for dz in (2, 1, 3):
+        first.exchange(dz)
+    first.spread[here.z] = first.mine[here.z]
     swap = remote(half, place, loads.at[5], loads.at[6], here.device(dc=1))
     swap.start()
+    for copy in fetch[2:]:
+        copy.start()
     turn(lengths, freqs, turns)
     fetch[0].wait()
     transposed(raw, weight_in)
@@ -509,11 +521,17 @@
     heads(c, first.owned, turns, qkv)
     fetch[2].wait()
     fetch[3].wait()
-    attend(lengths, keys, values, qkv, scored, weighed, mixed, second.mine)
+    first.finish_exchange()
+    for dz in (2, 1, 3, 0):
+        to = (here.z + dz) % 4
+        result = second.mine if dz else second.spread
+        attend(to, lengths, keys, values, qkv, scored, weighed, mixed, result)
+        if dz:
+            second.exchange(dz)
     first.finish()
-    second.exchange()
     second.run(fetch[4].wait)
     out[...] = second.owned[...]
+    second.finish_exchange()
     second.finish()
 
 
@@ -525,9 +543,14 @@
     blocks = pl.pallas_call(
         layer,
         out_shape=jax.ShapeDtypeStruct((32, ROWS, 512), jnp.bfloat16),
-        in_specs=[pl.BlockSpec(memory_space=pltpu.SMEM), vmem, vmem, vmem, hbm, hbm, hbm, hbm],
+        in_specs=[hbm] * 8,
         out_specs=vmem,
         scratch_shapes=[
+            pltpu.SMEM((ROWS,), jnp.int32),
+            pltpu.VMEM((ROWS, 4 * DEPTH), jnp.bfloat16),
+            pltpu.VMEM((1, 4 * DEPTH), jnp.float32),
+            pltpu.VMEM((1, HD), jnp.float32),
+            pltpu.SemaphoreType.DMA((4,)),
             pltpu.VMEM((1024, DEPTH), jnp.bfloat16),
             pltpu.VMEM((HD, DEPTH), jnp.bfloat16),
             pltpu.VMEM((DEPTH, 512), jnp.bfloat16),
@@ -536,9 +559,9 @@
             pltpu.VMEM((DEPTH, 512), jnp.bfloat16),
             pltpu.VMEM((2, ROWS, HD), jnp.float32),
             pltpu.VMEM(((HQ + 2 * KVH) * ROWS, HD), jnp.float32),
-            pltpu.VMEM((ROWS, HQ, CACHE), jnp.float32),
-            pltpu.VMEM((ROWS, HQ, CACHE), jnp.bfloat16),
-            pltpu.VMEM((HQ * ROWS, HD), jnp.float32),
+            pltpu.VMEM((ROWS, HQ // 4, CACHE), jnp.float32),
+            pltpu.VMEM((ROWS, HQ // 4, CACHE), jnp.bfloat16),
+            pltpu.VMEM((HQ // 4 * ROWS, HD), jnp.float32),
             pltpu.VMEM((1024, DEPTH), jnp.bfloat16),
             pltpu.SemaphoreType.DMA((7,)),
             pltpu.SemaphoreType.DMA((Projection.SEMAPHORES,)),

time: 111 us -> 100 us (0.901)
  Pallas kernels: 109 us -> 98.4 us
    pallas_call x1, Pallas kernels: 109 us -> 98.4 us  [on_device(): pl.pallas_call(layer, out_shape=jax.ShapeDtypeStruct((32, ROWS, 512), jnp...]
where the time goes in v6:
time: 100 us
  Pallas kernels  98.4 us (98%)
  local copies, waits for them, and re-layouts  1.67 us (2%)
    pallas_call x1, Pallas kernels, on_device(): pl.pallas_call(layer, out_shape=jax.ShapeDtypeStruct((32, ROWS, 512), jnp...  98.4 us

profile of v6, /device:TPU:1, one launch (start us, length us, event | category | flops | bytes accessed | tf_op | source)
XLA Modules:
  0.0 100.1 jit_solution(12344851215850084768)
XLA Ops:
  0.0 98.4 %layer.1 = bf16[32,8,512]{2,1,0:T(8,128)(2,1)} custom-call(s32[8]{0:T(128)} %lengths_in.1, bf16[8,16384]{1,0:T(8,128)(2,1)} %hidden_in.1, f32[1,16384]{1,0:T(1,128)} %bitcast.7, f32[1,128]{1,0:T(1,128)} %constant.2.clone.freqs_in, bf16[576,4096]{1,0:T(8,128)(2,1)} %bitcast.5, bf16[8,512,1024]{2,1,0:T(8,128)(2,1)} %k_cache.1, bf16[8,512,1024]{2,1,0:T(8,128)(2,1)} %v_cache.1, ...), custom_call_target="tpu_custom_call" | custom-call | tf_op jit(solution)/shard_map/layer/pallas_call | solution.py:543
  98.4 1.7 %copy.10 = bf16[8,16384]{1,0:T(8,128)(2,1)} copy(bf16[8,16384]{1,0:T(8,128)(2,1)} %bitcast.6) | data formatting | bytes 524288

commit v7 on v6

--- a/solution.py
+++ b/solution.py
@@ -530,7 +530,7 @@
             second.exchange(dz)
     first.finish()
     second.run(fetch[4].wait)
-    out[...] = second.owned[...]
+    out[...] = second.owned[...].astype(jnp.float32)
     second.finish_exchange()
     second.finish()
 
@@ -542,7 +542,7 @@
     hbm = pl.BlockSpec(memory_space=pl.ANY)
     blocks = pl.pallas_call(
         layer,
-        out_shape=jax.ShapeDtypeStruct((32, ROWS, 512), jnp.bfloat16),
+        out_shape=jax.ShapeDtypeStruct((32, ROWS, 512), jnp.float32),
         in_specs=[hbm] * 8,
         out_specs=vmem,
         scratch_shapes=[
@@ -573,7 +573,7 @@
         ),
         name="layer",
     )(lengths, hidden_in, norm_gain.reshape(1, -1), freqs, w_qkv.T, k_cache, v_cache, w_out)
-    return blocks.transpose(1, 0, 2).reshape(ROWS, 32 * 512)
+    return blocks.transpose(1, 0, 2).reshape(ROWS, 32 * 512).astype(jnp.bfloat16)
 
 
 def solution(mesh):

time: 100 us -> 100 us (level)
  other arithmetic: 0 us -> 1.78 us
  local copies, waits for them, and re-layouts: 1.67 us -> 0 us
    convert_element_type x0 -> x1, other arithmetic: none -> 1.78 us  [on_device(): blocks.transpose(1, 0, 2).reshape(ROWS, 32 * 512).astype(jnp.bfloat16)]
    unnamed x1 -> x0, local copies, waits for them, and re-layouts: 1.67 us -> none
where the time goes in v7:
time: 100 us
  Pallas kernels  98.5 us (98%)
  other arithmetic  1.78 us (2%)
    pallas_call x1, Pallas kernels, on_device(): pl.pallas_call(layer, out_shape=jax.ShapeDtypeStruct((32, ROWS, 512), jnp...  98.5 us

profile of v7, /device:TPU:1, one launch (start us, length us, event | category | flops | bytes accessed | tf_op | source)
XLA Modules:
  0.0 100.3 jit_solution(4139900766487023864)
XLA Ops:
  0.0 98.5 %layer.1 = f32[32,8,512]{2,1,0:T(8,128)} custom-call(s32[8]{0:T(128)} %lengths_in.1, bf16[8,16384]{1,0:T(8,128)(2,1)} %hidden_in.1, f32[1,16384]{1,0:T(1,128)} %bitcast.6, f32[1,128]{1,0:T(1,128)} %constant.2.clone.freqs_in, bf16[576,4096]{1,0:T(8,128)(2,1)} %bitcast.5, bf16[8,512,1024]{2,1,0:T(8,128)(2,1)} %k_cache.1, bf16[8,512,1024]{2,1,0:T(8,128)(2,1)} %v_cache.1, ...), custom_call_target="tpu_custom_call" | custom-call | tf_op jit(solution)/shard_map/layer/pallas_call | solution.py:543
  98.5 1.8 %convert_element_type.9 = bf16[32,8,512]{2,1,0:T(8,128)(2,1)} convert(f32[32,8,512]{2,1,0:T(8,128)} %layer.1) | non-fusion elementwise | flops 131072 | bytes 786432 | tf_op jit(solution)/shard_map/convert_element_type | solution.py:576
